TPU v7x, 256 devices: a whole 4x4x8 slice. The times are simulated.
256 devices in a mesh: fsdp: 16 (over z, core), rep: 16 (over y, x).
Axes of the slice: x: 4, y: 4, z: 8, core: 2. Of those that a mesh axis runs over, the one named last changes fastest.
Arguments:
- inputs: bfloat16 [32768, 256], P(('fsdp', 'rep')), may hold values from -6 to 6
- cotangent: bfloat16 [32768, 28672], P(('fsdp', 'rep')), may hold values from -0.5 to 0.5
- momentum: float32 [16, 28672, 256], P('rep', 'fsdp'), may hold values from -12 to 12
- coef_index: int32 [16, 448, 4, 32], P('rep', 'fsdp'), may hold values from 0 to 4095, as said below
- counts: int32 [16, 448, 4], P('rep', 'fsdp'), may hold values from 8 to 32, as said below
Outputs:
- new_momentum: float32 [16, 28672, 256], P('rep', 'fsdp')
- update: float32 [28672, 256], P('fsdp')
Inputs may be any that keep to these rules, and one draw needn't show every extreme that they name: `coef_index`: the 32 frequencies listed for one group of one replica are all different. `counts`: every replica has a group with all 32 slots valid.
All inputs are finite; a program needn't handle non-finite values.
Results may differ from a plain program's by a relative error of at most 0.0003.
Values may be sent and summed in bfloat16 or wider, within the bound.
No kernel may reach another device: no remote copies, remote signals or barrier semaphores. Data moves between devices by JAX's collectives and lax.ppermute only.
A program may use at most 128 MiB of HBM per device.

v0:
```python
import math

import jax
import jax.numpy as jnp
from jax import lax
from jax.sharding import PartitionSpec as P

GROUP = 64


decay_rate = 0.9


def cosine_table(group_size):
    freq = jnp.arange(group_size, dtype=jnp.float32)[:, None]
    place_ids = jnp.arange(group_size, dtype=jnp.float32)[None, :]
    cosines = jnp.cos(math.pi * (2.0 * place_ids + 1.0) * freq / (2.0 * group_size)) * math.sqrt(
        2.0 / group_size
    )
    scaling = jnp.where(jnp.arange(group_size) == 0, math.sqrt(0.5), 1.0).astype(cosines.dtype)
    return cosines * scaling[:, None]


def forward_groups(matrix_tile, cosines):
    group_size = cosines.shape[0]
    height, width = matrix_tile.shape
    grouped = matrix_tile.reshape(height // group_size, group_size, width // group_size, group_size)
    spectrum = jnp.einsum(
        "un,anbm,wm->abuw", cosines, grouped, cosines, precision=lax.Precision.HIGHEST
    )
    return spectrum.reshape(height // group_size, width // group_size, group_size * group_size)


def inverse_groups(spectrum, cosines):
    group_size = cosines.shape[0]
    across, down_count, _ = spectrum.shape
    square = spectrum.reshape(across, down_count, group_size, group_size)
    grouped = jnp.einsum(
        "un,abuw,wm->anbm", cosines, square, cosines, precision=lax.Precision.HIGHEST
    )
    return grouped.reshape(across * group_size, down_count * group_size)


def on_device(inputs, cotangent, momentum, coef_index, counts):
    cosines = cosine_table(GROUP)
    gradient = lax.psum_scatter(
        lax.dot_general(
            cotangent, inputs, (((0,), (0,)), ((), ())), preferred_element_type=jnp.float32
        ),
        "fsdp",
        scatter_dimension=0,
        tiled=True,
    )
    updated = decay_rate * momentum[0] + gradient
    own_index = coef_index[0]
    own_counts = counts[0]
    spectrum = forward_groups(updated, cosines)
    picked = jnp.take_along_axis(spectrum, own_index, axis=2)
    slot_ids = jnp.arange(picked.shape[2], dtype=jnp.int32)[None, None, :]
    kept_values = jnp.where(slot_ids < own_counts[:, :, None], picked, 0.0)
    across, down_count, slot_count = own_index.shape
    total_slots = spectrum.shape[2]
    group_ids = jnp.arange(across * down_count, dtype=jnp.int32)[:, None]
    own_dense = jnp.zeros((across * down_count, total_slots), jnp.float32)
    own_dense = own_dense.at[group_ids, own_index.reshape(across * down_count, slot_count)].add(
        kept_values.reshape(across * down_count, slot_count)
    )
    decoded_own = inverse_groups(own_dense.reshape(across, down_count, total_slots), cosines)
    new_momentum = (updated - decoded_own)[None]
    update = lax.psum(decoded_own, "rep")
    return (new_momentum, update)


def solution(mesh):
    return jax.shard_map(
        on_device,
        mesh=mesh,
        in_specs=(
            P(("fsdp", "rep"), None),
            P(("fsdp", "rep"), None),
            P("rep", "fsdp", None),
            P("rep", "fsdp", None, None),
            P("rep", "fsdp", None),
        ),
        out_specs=(P("rep", "fsdp", None), P("fsdp", None)),
        check_vma=False,
    )
```

profile of v0, /device:TPU:24, one launch (start us, length us, event | category | flops | bytes accessed | tf_op | source)
XLA Modules:
  0.0 400.3 jit_solution(1875090680093342586)
XLA Ops:
  7.2 0.8 copy-done
  8.0 16.8 %fusion.30 = f32[28672,256]{1,0:T(8,128)} fusion(bf16[128,28672]{1,0:T(8,128)(2,1)} %param.6, bf16[128,256]{1,0:T(8,128)(2,1)S(1)} %copy-done), kind=kOutput, calls=%fused_computation.47 | convolution fusion | flops 1879048192 | bytes 36765696 | tf_op jit(solution)/shard_map/dot_general | solution.py:47
  24.8 0.8 copy-done.4
  25.9 0.1 copy.25
  26.1 0.1 reshape.109
  26.2 0.1 copy.26
  26.3 0.1 lt.56
  26.4 165.4 %reduce-scatter.2.cloned.1.call-done = f32[1792,256]{1,0:T(8,128)} async-done(((f32[28672,256]{1,0:T(8,128)}), f32[1792,256]{1,0:T(8,128)}) %reduce-scatter.2.cloned.1.call-update) | async-done | bytes 1835024 | tf_op jit(solution)/shard_map/reduce_scatter | solution.py:46
  191.8 2.3 bitcast_add_fusion
  194.1 3.0 reshape.101
  197.1 5.7 %fusion = f32[28,4,64,64]{2,3,1,0:T(8,128)S(1)} fusion(f32[28,64,4,64]{3,2,1,0:T(4,128)} %reshape.101, f32[64]{0:T(128)S(1)} %get-tuple-element.2, f32[64]{0:T(128)S(1)} %get-tuple-element.3), kind=kOutput, calls=%fused_computation.2 | convolution fusion | flops 352333824 | bytes 3670528 | tf_op jit(solution)/shard_map/un,anbm,wm->abuw/dot_general | solution.py:28
  202.8 4.9 %fusion.10 = f32[28,4,64,64]{3,2,1,0:T(8,128)} fusion(f32[28,4,64,64]{2,3,1,0:T(8,128)S(1)} %fusion, f32[64]{0:T(128)S(1)} %get-tuple-element.2, f32[64]{0:T(128)S(1)} %get-tuple-element.3), kind=kOutput, calls=%fused_computation.21 | convolution fusion | flops 352333824 | bytes 3670528 | tf_op jit(solution)/shard_map/un,anbm,wm->abuw/dot_general | solution.py:28
  207.7 3.5 reshape.102
  211.2 33.9 %gather_fusion = f32[3584]{0:T(1024)S(1)} fusion(f32[28,4,4096]{2,1,0:T(4,128)S(1)} %reshape.102, s32[3584]{0:T(1024)S(1)} %reshape.109), kind=kCustom, calls=%fused_computation | custom fusion | bytes 71680 | tf_op jit(solution)/shard_map/jit(take_along_axis)/gather | solution.py:58
  245.4 19.7 %scatter_custom_fusion = f32[458752]{0:T(1024)S(1)} fusion(s32[3584]{0:T(1024)S(1)} %reshape.115, f32[3584]{0:T(1024)S(1)} %reshape.117, f32[]{:T(128)} %constant.13.clone.1), kind=kCustom, calls=%fused_computation.7 | custom fusion | flops 3584 | bytes 1835012
  265.0 2.3 reshape_reshape.3
  267.4 5.7 %fusion.8 = f32[28,4,64,64]{2,3,1,0:T(8,128)S(1)} fusion(f32[28,4,64,64]{3,2,1,0:T(8,128)} %reshape_reshape.3, f32[64]{0:T(128)S(1)} %get-tuple-element.2, f32[64]{0:T(128)S(1)} %get-tuple-element.3), kind=kOutput, calls=%fused_computation.19 | convolution fusion | flops 352333824 | bytes 3670528 | tf_op jit(solution)/shard_map/un,abuw,wm->anbm/dot_general | solution.py:38
  273.1 3.3 convolution_bitcast_fusion
  276.4 4.8 %copy.31 = f32[28,64,4,64]{3,2,1,0:T(4,128)} copy(f32[28,64,4,64]{3,1,2,0:T(8,128)S(1)} %convolution_bitcast_fusion) | data formatting | bytes 3670016 | tf_op jit(solution)/shard_map/un,abuw,wm->anbm/transpose | solution.py:38
  281.2 3.7 reshape.103
  285.0 3.6 subtract_bitcast_fusion
  288.6 0.7 all-reduce.2.cloned.1.call-update
  289.4 101.2 %all-reduce.2.cloned.1.call-done = f32[1792,256]{1,0:T(8,128)} async-done(((f32[1792,256]{1,0:T(8,128)}), f32[1792,256]{1,0:T(8,128)}) %all-reduce.2.cloned.1.call-update) | async-done | bytes 1835024 | tf_op jit(solution)/shard_map/psum | solution.py:70
  390.6 2.8 copy.39
  (29 shorter events, 0.7 us)
Async XLA Ops:
  7.2 0.8 copy-start
  7.2 184.6 %reduce-scatter.2.cloned.1.call-start = ((), (), s32[]{:S(2)}) async-start(), calls=%async_computation.1 | async-start | bytes 31195136 | tf_op jit(solution)/shard_map/reduce_scatter | solution.py:46
  24.8 0.8 copy-start.4
  24.8 0.9 copy-start.6
  24.8 1.0 copy-start.7
  24.8 1.4 copy-start.5
  194.1 3.0 copy-start.3
  285.0 3.6 copy-start.2
  288.6 102.0 %all-reduce.2.cloned.1.call-start = ((), (), s32[]{:S(2)}) async-start(), calls=%async_computation.2 | async-start | bytes 3670016 | tf_op jit(solution)/shard_map/psum | solution.py:70
  289.3 104.1 %copy-start.1 = (bf16[128,256]{1,0:T(8,128)(2,1)S(1)}, bf16[128,256]{1,0:T(8,128)(2,1)}, u32[]{:S(2)}) copy-start(bf16[128,256]{1,0:T(8,128)(2,1)} %param.5) | copy-start | bytes 196612
Sparse Core Ops, SparseCore 0:
  24.9 166.8 reduce-scatter.1
  292.8 97.7 all-reduce.1
where the time goes:
time: 401 us; the launch traced here: 400 us
  waiting for transfers between devices  267 us (67%)
  local copies, waits for them, and re-layouts  56.4 us (14%)
  matrix products  36.4 us (9%)
  other arithmetic  25.9 us (6%)
  between operations  14.2 us (4%)
    reduce_scatter x1, waiting for transfers between devices, on_device(): lax.psum_scatter(lax.dot_general(cotangent, inputs, (((0,), (0,)), ((), (...  165 us
    psum x1, waiting for transfers between devices, on_device(): update = lax.psum(decoded_own, 'rep')  101 us
    gather x3, local copies, waits for them, and re-layouts, on_device(): picked = jnp.take_along_axis(spectrum, own_index, axis=2)  34.1 us
    unnamed x4, other arithmetic  19.8 us
    dot_general x1, matrix products, on_device(): lax.dot_general(cotangent, inputs, (((0,), (0,)), ((), ())), preferred_el...  16.8 us
    dot_general x2, matrix products, forward_groups(): jnp.einsum('un,anbm,wm->abuw', cosines, grouped, cosines, precision=lax.P...  10.6 us
    dot_general x2, matrix products, inverse_groups(): jnp.einsum('un,abuw,wm->anbm', cosines, square, cosines, precision=lax.Pr...  9.02 us
  transfers between devices with their start and end apart: 2, of which 2 were waited for; matrix products, arithmetic and copies ran while one was open for 0% of the time, Pallas kernels for 0%

commit v1 on v0

v1 whole, which is shorter than its diff:
```python
import functools
import math

import jax
import jax.numpy as jnp
import numpy as np
from jax import lax
from jax.experimental import pallas as pl
from jax.experimental.pallas import tpu as pltpu
from jax.sharding import PartitionSpec as P

GROUP = 64
DECAY = 0.9
CHIPS = 8
TOK = 128
COLS = 256
ROWS = 1792
HALF = 896
TILES = ROWS // 128
GROUPS = ROWS // GROUP
HALF_GROUPS = GROUPS // 2
GROUPS = ROWS // GROUP
HALF_GROUPS = GROUPS // 2
MSG = TILES * COLS + 16
N_REP = 16
STEP = 64.0
TOP = 32760.0
HIGH = lax.Precision.HIGHEST
F32 = jnp.float32
BF16 = jnp.bfloat16
SLOTS = (
    (4, False),
    (3, True),
    (3, False),
    (2, True),
    (2, False),
    (1, True),
    (1, False),
    (0, False),
)
VMEM_LIMIT = 24 * 1024 * 1024


def cosine_table():
    freq = np.arange(GROUP)[:, None]
    place = np.arange(GROUP)[None, :]
    table = np.cos(math.pi * (2.0 * place + 1.0) * freq / (2.0 * GROUP)) * math.sqrt(2.0 / GROUP)
    table[0] *= math.sqrt(0.5)
    return table.astype(np.float32)


def call(kernel, out_shape, name, grid, in_specs, out_specs, scalars=0, scratch=(), flops=235_000_000, nbytes=1_400_000):
    return pl.pallas_call(
        kernel,
        out_shape=out_shape,
        name=name,
        grid_spec=pltpu.PrefetchScalarGridSpec(
            num_scalar_prefetch=scalars,
            grid=grid,
            in_specs=in_specs,
            out_specs=out_specs,
            scratch_shapes=scratch,
        ),
        compiler_params=pltpu.CompilerParams(vmem_limit_bytes=VMEM_LIMIT),
        cost_estimate=pl.CostEstimate(flops=flops, bytes_accessed=nbytes, transcendentals=0),
    )


def whole(*shape):
    return pl.BlockSpec(shape, lambda *_: (0,) * len(shape))


AFTER = pl.BlockSpec(memory_space=pl.ANY)


def split(x):
    high = x.astype(BF16)
    return high, (x - high.astype(F32)).astype(BF16)


def read_scales(msg):
    codes = msg[TILES * COLS : MSG, :].astype(F32)
    return jnp.exp2(codes * (1.0 / STEP)) * (1.0 / TOP)


def read_tile(msg, scales, j):
    return msg[j * COLS : (j + 1) * COLS, :].astype(F32) * scales[j : j + 1, :]


def partial_tile(in_t, own, sib, j):
    cols = slice(j * 128, (j + 1) * 128)
    tokens = jnp.concatenate([own[:, cols], sib[:, cols]], axis=0)
    return jnp.dot(in_t, tokens, preferred_element_type=F32)


def write_message(out, tiles):
    codes = []
    for j, tile in enumerate(tiles):
        top = jnp.maximum(jnp.max(jnp.abs(tile), axis=0, keepdims=True), 1e-30)
        code = jnp.ceil(jnp.log2(top) * STEP)
        inv = jnp.exp2(code * (-1.0 / STEP)) * TOP
        out[j * COLS : (j + 1) * COLS, :] = jnp.round(tile * inv).astype(jnp.int32).astype(jnp.int16)
        codes.append(code)
    codes.append(jnp.zeros((16 - len(codes), 128), F32))
    out[TILES * COLS : MSG, :] = jnp.concatenate(codes, axis=0).astype(jnp.int32).astype(jnp.int16)


def copy_kernel(slots, cot, extra, send, own, sems):
    place = lax.axis_index("fsdp")
    chip, core = place // 2, place % 2
    copies = []
    for whose, out in ((1 - core, send), (core, own)):
        for n, (k, flip) in enumerate(slots if out is not None else ()):
            to = (chip + k * (1 - 2 * whose) + CHIPS) % CHIPS
            start = pl.multiple_of((2 * to + (1 - whose if flip else whose)) * ROWS, 128)
            for row in range(0, TOK, 32):
                rows = slice(row, row + 32)
                copies.append(
                    (
                        cot.at[rows, pl.ds(start, ROWS)],
                        out.at[rows, n * ROWS : (n + 1) * ROWS],
                        sems.at[len(copies)],
                    )
                )
    copies = [pltpu.make_async_copy(*c) for c in copies]
    for c in copies:
        c.start()
    if extra is not None:
        send[:, len(slots) * ROWS :] = extra[...]
    for c in copies:
        c.wait()


def first_copy_kernel(cot, extra, send, own, sems):
    copy_kernel(SLOTS[:1], cot, extra, send, own, sems)


def later_copy_kernel(slots, cot, after, send, own, sems):
    copy_kernel(slots, cot, None, send, own, sems)


def first_hop_kernel(in_own, in_sib, own, sib, after, in_t, out):
    in_t[:, :TOK] = in_own[...].astype(F32).T.astype(BF16)
    in_t[:, TOK:] = in_sib[...].astype(F32).T.astype(BF16)
    both = in_t[...]
    write_message(out, [partial_tile(both, own, sib, j) for j in range(TILES)])


def hop_kernel(n_after, *refs):
    in_t, own, sib, *recv, out = refs[n_after:]
    both = in_t[...]
    tiles = [partial_tile(both, own, sib, j) for j in range(TILES)]
    if recv:
        scales = read_scales(recv[0])
        tiles = [tile + read_tile(recv[0], scales, j) for j, tile in enumerate(tiles)]
    write_message(out, tiles)


def tables_kernel(listed, counts, cos_t, after, basis, cw, valid, places):
    row = lax.broadcasted_iota(jnp.int32, (GROUP, 512), 0)
    lane = lax.broadcasted_iota(jnp.int32, (GROUP, 256), 1)
    index = jnp.concatenate([listed[:, j, :] for j in range(4)], axis=1)
    places[...] = index.astype(F32)
    for p in range(TILES):
        n = jnp.concatenate([index[2 * p : 2 * p + 1, :], index[2 * p + 1 : 2 * p + 2, :]], axis=1)
        onehot = jnp.where(row == jnp.concatenate([n >> 6, n & 63], axis=1), 1.0, 0.0).astype(F32)
        both = jnp.dot(cos_t[...], onehot, precision=HIGH, preferred_element_type=F32)
        cw[p * GROUP : (p + 1) * GROUP, :] = both[:, 256:]
        cu = both[:, :256]
        diagonal = jnp.concatenate(
            [jnp.where(lane < 128, cu, 0.0), jnp.where(lane >= 128, cu, 0.0)], axis=0
        )
        high, low = split(diagonal)
        basis[p * 256 : p * 256 + 128, :] = high
        basis[p * 256 + 128 : (p + 1) * 256, :] = low
    slot = lax.broadcasted_iota(jnp.int32, (GROUPS, 128), 1)
    limit = jnp.zeros((GROUPS, 128), jnp.int32)
    for j in range(4):
        limit = jnp.where((slot >> 5) == j, counts[:, j : j + 1], limit)
    valid[...] = jnp.where((slot & 31) < limit, 1.0, 0.0).astype(F32)


def momentum_kernel(momentum, after, out):
    out[...] = (DECAY * momentum[...]).T


def by_column_group(rows):
    block = lax.broadcasted_iota(jnp.int32, rows[0].shape, 1) >> 5
    out = []
    for j in range(4):
        total = rows[j]
        for b in range(4):
            if b != j:
                total = jnp.where(block == b, pltpu.roll(rows[b], (32 * (b - j)) % 128, 1), total)
        out.append(total)
    return out


def base_kernel(in_t, own, sib, msg, mom_t, out):
    both = in_t[...]
    scales = read_scales(msg)
    for j in range(TILES):
        cols = slice(j * 128, (j + 1) * 128)
        out[:, cols] = partial_tile(both, own, sib, j) + mom_t[:, cols] + read_tile(msg, scales, j)


def kept_kernel(msg, base, basis, cw, valid, places, updated, kept):
    kept[GROUPS:, :] = places[...]
    column = (lax.broadcasted_iota(jnp.int32, (GROUP, 256), 1) & 127) >> 5
    scales = read_scales(msg)
    for p in range(TILES):
        cols = slice(p * 128, (p + 1) * 128)
        tile = base[:, cols] + read_tile(msg, scales, p)
        updated[:, cols] = tile
        high, low = split(tile)
        b_high = basis[p * 256 : p * 256 + 128, :]
        b_low = basis[p * 256 + 128 : (p + 1) * 256, :]
        seen = jnp.dot(
            jnp.concatenate([high, low, high], axis=1),
            jnp.concatenate([b_high, b_high, b_low], axis=0),
            preferred_element_type=F32,
        )
        mine = seen[:GROUP]
        for c in range(1, 4):
            mine = jnp.where(column == c, seen[c * GROUP : (c + 1) * GROUP], mine)
        picked = jnp.sum(mine * cw[p * GROUP : (p + 1) * GROUP, :], axis=0, keepdims=True)
        for i in range(2):
            at = slice(2 * p + i, 2 * p + i + 1)
            half = picked[:, i * 128 : (i + 1) * 128]
            kept[at, :] = jnp.where(valid[at, :] > 0.0, half, 0.0)


def own_kernel(updated, kept, basis, cw, out):
    g = pl.program_id(0)
    column = (lax.broadcasted_iota(jnp.int32, (GROUP, 256), 1) & 127) >> 5
    for p in range(TILES // 2):
        k = jnp.concatenate(
            [kept[pl.ds(2 * (g * (TILES // 2) + p) + i, 1), :] for i in range(2)], axis=1
        )
        weighted = cw[p * GROUP : (p + 1) * GROUP, :] * k
        spread = jnp.concatenate([jnp.where(column == c, weighted, 0.0) for c in range(4)], axis=0)
        high, low = split(spread)
        b_high = basis[p * 256 : p * 256 + 128, :]
        b_low = basis[p * 256 + 128 : (p + 1) * 256, :]
        decoded = lax.dot_general(
            jnp.concatenate([high, low, high], axis=1),
            jnp.concatenate([b_high, b_high, b_low], axis=1),
            (((1,), (1,)), ((), ())),
            preferred_element_type=F32,
        )
        cols = slice(p * 128, (p + 1) * 128)
        out[cols, :] = (updated[:, cols] - decoded).T


def update_kernel(k0, k1, k2, k3, cos_t3, cos4_3, out, kept, index):
    g = pl.program_id(0)

    @pl.when(g == 0)
    def _():
        for y, ref in enumerate((k0, k1, k2, k3)):
            for rows, arranged in ((slice(0, GROUPS), kept), (slice(GROUPS, 2 * GROUPS), index)):
                groups = by_column_group([ref[x, rows, :] for x in range(4)])
                for j in range(4):
                    arranged[j, y] = groups[j]

    row = lax.broadcasted_iota(jnp.int32, (GROUP, 512), 0).astype(F32).astype(BF16)
    one, zero = jnp.ones((GROUP, 512), BF16), jnp.zeros((GROUP, 512), BF16)
    dense = []
    for i in range(HALF_GROUPS):
        at = pl.ds(g * HALF_GROUPS + i, 1)
        for j in range(4):
            k = jnp.concatenate([kept[j, y, at, :] for y in range(4)], axis=1)
            n = jnp.concatenate([index[j, y, at, :] for y in range(4)], axis=1).astype(jnp.int32)
            high, low = split(k)
            here = row == (n >> 6).astype(F32).astype(BF16)
            left = jnp.concatenate(
                [jnp.where(here, high, zero), jnp.where(here, low, zero)], axis=0
            )
            right = jnp.where(row == (n & 63).astype(F32).astype(BF16), one, zero)
            both = lax.dot_general(
                left, right, (((1,), (1,)), ((), ())), preferred_element_type=F32
            )
            dense.append(both[:GROUP] + both[GROUP:])
    high, low = split(jnp.concatenate(dense, axis=1))
    half = jnp.dot(
        cos_t3[...], jnp.concatenate([high, low, high], axis=0), preferred_element_type=F32
    )
    half = jnp.concatenate([half[:, i * 256 : (i + 1) * 256] for i in range(HALF_GROUPS)], axis=0)
    high, low = split(half)
    out[...] = jnp.dot(
        jnp.concatenate([high, low, high], axis=1), cos4_3[...], preferred_element_type=F32
    )


def ring_perm(flip):
    return [
        (2 * z + c, 2 * ((z + 1 - 2 * c) % CHIPS) + (1 - c if flip else c))
        for z in range(CHIPS)
        for c in range(2)
    ]


def rep_perm(dx, dy):
    return [(i, ((i // 4 + dy) % 4) * 4 + (i % 4 + dx) % 4) for i in range(N_REP)]


def on_device(inputs, cotangent, momentum, coef_index, counts):
    cosines = cosine_table()
    cos_t = jnp.asarray(cosines.T)
    parts = lambda x: (x.astype(BF16), (x - x.astype(BF16).astype(np.float32)).astype(BF16))
    high, low = parts(cosines.T)
    cos_t3 = jnp.asarray(np.concatenate([high, high, low], axis=1))
    high, low = parts(np.kron(np.eye(4, dtype=np.float32), cosines))
    cos4_3 = jnp.asarray(np.concatenate([high, high, low], axis=0))

    swap = lambda x: lax.ppermute(x, "fsdp", [(i, i ^ 1) for i in range(2 * CHIPS)])
    own_of, theirs_of = [], []

    def copied(begin, end, after, name):
        n = end - begin
        extra = COLS if begin == 0 else 0
        send, own = call(
            functools.partial(later_copy_kernel, SLOTS[begin:end]) if begin else first_copy_kernel,
            (
                jax.ShapeDtypeStruct((TOK, n * ROWS + extra), BF16),
                jax.ShapeDtypeStruct((TOK, n * ROWS), BF16),
            ),
            name,
            (1,),
            [AFTER, AFTER if begin else whole(TOK, COLS)],
            (whole(TOK, n * ROWS + extra), whole(TOK, n * ROWS)),
            scratch=[pltpu.SemaphoreType.DMA((8 * n,))],
        )(cotangent, after)
        theirs = swap(send)
        own_of.extend((own, i) for i in range(n))
        theirs_of.extend((theirs, i) for i in range(n))
        return send, theirs

    first, first_theirs = copied(0, 1, inputs, "copy0")
    second, _ = copied(1, 3, first, "copy12")

    def blocks(slot):
        specs, args = [], []
        for array, n in (own_of[slot], theirs_of[slot]):
            specs.append(pl.BlockSpec((TOK, ROWS), lambda *_, n=n: (0, n)))
            args.append(array)
        return specs, args

    message = jax.ShapeDtypeStruct((MSG, 128), jnp.int16)

    def made_tables(after):
        return call(
            tables_kernel,
            (
                jax.ShapeDtypeStruct((TILES * 256, 256), BF16),
                jax.ShapeDtypeStruct((TILES * GROUP, 256), F32),
                jax.ShapeDtypeStruct((GROUPS, 128), F32),
                jax.ShapeDtypeStruct((GROUPS, 128), F32),
            ),
            "tables",
            (1,),
            [whole(GROUPS, 4, 32), whole(GROUPS, 4), whole(GROUP, GROUP), AFTER],
            (whole(TILES * 256, 256), whole(TILES * GROUP, 256)) + (whole(GROUPS, 128),) * 2,
        )(coef_index[0], counts[0], cos_t, after)

    def momentum_t(momentum, after):
        return call(
            momentum_kernel,
            jax.ShapeDtypeStruct((COLS, ROWS), F32),
            "momentum",
            (2,),
            [pl.BlockSpec((HALF, COLS), lambda g: (g, 0)), AFTER],
            pl.BlockSpec((COLS, HALF), lambda g: (0, g)),
        )(momentum, after)

    made, sent = [], []
    for slot in range(7):
        if slot == 1:
            copied(3, 5, made[0], "copy34")
        if slot == 3:
            copied(5, 8, made[2], "copy567")
        specs, args = blocks(slot)
        if slot == 0:
            in_t, out = call(
                first_hop_kernel,
                (jax.ShapeDtypeStruct((COLS, 2 * TOK), BF16), message),
                "hop0",
                (1,),
                [whole(TOK, COLS), pl.BlockSpec((TOK, COLS), lambda g: (0, ROWS // COLS))]
                + specs
                + [AFTER],
                (whole(COLS, 2 * TOK), whole(MSG, 128)),
            )(inputs, first_theirs, *args, second)
        else:
            recv = sent[slot - 2 : slot - 1]
            after = (made[-1],)
            if slot == 3:
                basis, cw, valid, places = made_tables(made[2])
            if slot == 4:
                after = (made[-1], basis)
                mom_t = momentum_t(momentum[0], made[3])
            if slot == 5:
                after = (made[-1], mom_t)
            out = call(
                functools.partial(hop_kernel, len(after)),
                message,
                "hop%d" % slot,
                (1,),
                [AFTER] * len(after)
                + [whole(COLS, 2 * TOK)]
                + specs
                + [whole(MSG, 128)] * len(recv),
                whole(MSG, 128),
            )(*after, in_t, *args, *recv)
        made.append(out)
        sent.append(lax.ppermute(out, "fsdp", ring_perm(slot == 5)))

    specs, args = blocks(7)
    base = call(
        base_kernel,
        jax.ShapeDtypeStruct((COLS, ROWS), F32),
        "base",
        (1,),
        [whole(COLS, 2 * TOK)] + specs + [whole(MSG, 128), whole(COLS, ROWS)],
        whole(COLS, ROWS),
    )(in_t, *args, sent[5], mom_t)
    updated, kept = call(
        kept_kernel,
        (
            jax.ShapeDtypeStruct((COLS, ROWS), F32),
            jax.ShapeDtypeStruct((2 * GROUPS, 128), F32),
        ),
        "kept",
        (1,),
        [
            whole(MSG, 128),
            whole(COLS, ROWS),
            whole(TILES * 256, 256),
            whole(TILES * GROUP, 256),
            whole(GROUPS, 128),
            whole(GROUPS, 128),
        ],
        (whole(COLS, ROWS), whole(2 * GROUPS, 128)),
    )(sent[6], base, basis, cw, valid, places)
    along_x = jnp.stack(
        [kept] + [lax.ppermute(kept, "rep", rep_perm(dx, 0)) for dx in (1, 2, 3)]
    )
    kept_all = [along_x] + [lax.ppermute(along_x, "rep", rep_perm(0, dy)) for dy in (1, 2, 3)]

    new_momentum = call(
        own_kernel,
        jax.ShapeDtypeStruct((ROWS, COLS), F32),
        "own",
        (2,),
        [
            pl.BlockSpec((COLS, HALF), lambda g: (0, g)),
            whole(2 * GROUPS, 128),
            pl.BlockSpec((TILES * 128, 256), lambda g: (g, 0)),
            pl.BlockSpec((TILES * GROUP // 2, 256), lambda g: (g, 0)),
        ],
        pl.BlockSpec((HALF, COLS), lambda g: (g, 0)),
    )(updated, kept, basis, cw)

    update = call(
        update_kernel,
        jax.ShapeDtypeStruct((ROWS, COLS), F32),
        "update",
        (2,),
        [whole(4, 2 * GROUPS, 128)] * 4 + [whole(GROUP, 3 * GROUP), whole(3 * COLS, COLS)],
        pl.BlockSpec((HALF, COLS), lambda g: (g, 0)),
        scratch=[pltpu.VMEM((4, 4, GROUPS, 128), F32)] * 2,
    )(*kept_all, cos_t3, cos4_3)
    return new_momentum[None], update


def solution(mesh):
    return jax.shard_map(
        on_device,
        mesh=mesh,
        in_specs=(
            P(("fsdp", "rep"), None),
            P(("fsdp", "rep"), None),
            P("rep", "fsdp", None),
            P("rep", "fsdp", None, None),
            P("rep", "fsdp", None),
        ),
        out_specs=(P("rep", "fsdp", None), P("fsdp", None)),
        check_vma=False,
    )
```

time: 401 us -> 110 us (0.27)
  waiting for transfers between devices: 267 us -> 55.3 us
  local copies, waits for them, and re-layouts: 56.4 us -> 5.26 us
  matrix products: 36.4 us -> 0 us
  Pallas kernels: 0 us -> 31.2 us
  other arithmetic: 25.9 us -> 0.01 us
  starting transfers between devices: 0.04 us -> 17.5 us
  between operations: 14.2 us -> 0.88 us
    reduce_scatter x1 -> x0, waiting for transfers between devices: 165 us -> none  [on_device(): lax.psum_scatter(lax.dot_general(cotangent, inputs, (((0,), (0,)), ((), (...]
    psum x1 -> x0, waiting for transfers between devices: 101 us -> none  [on_device(): update = lax.psum(decoded_own, 'rep')]
    ppermute x0 -> x17, waiting for transfers between devices: none -> 55.3 us  [the longest x7 47.7 us: on_device(): sent.append(lax.ppermute(out, 'fsdp', ring_perm(slot == 5)))]
    dot_general x5 -> x0, matrix products: 36.4 us -> none  [the longest x1 16.8 us: on_device(): lax.dot_general(cotangent, inputs, (((0,), (0,)), ((), ())), preferred_el...]
    gather x3 -> x0, local copies, waits for them, and re-layouts: 34.1 us -> none  [on_device(): picked = jnp.take_along_axis(spectrum, own_index, axis=2)]
    pallas_call x0 -> x17, Pallas kernels: none -> 31.2 us  [the longest x6 9.78 us: on_device(): call(functools.partial(hop_kernel, len(after)), message, 'hop%d' % slot,...]
    unnamed x4 -> x1, other arithmetic: 19.8 us -> 0.01 us
    ppermute x0 -> x17, starting transfers between devices: none -> 17.5 us  [the longest x4 5.46 us: on_device(): lax.ppermute(x, 'fsdp', [(i, i ^ 1) for i in range(2 * CHIPS)])]
  transfers between devices with their start and end apart: 2 -> 17, of which waited for: 2 -> 12; matrix products, arithmetic and copies ran while one was open for 0% -> 0% of each run, Pallas kernels for 0% -> 21%
where the time goes in v1:
time: 110 us
  waiting for transfers between devices  55.3 us (50%)
  Pallas kernels  31.2 us (28%)
  starting transfers between devices  17.5 us (16%)
  local copies, waits for them, and re-layouts  5.26 us (5%)
    ppermute x7, waiting for transfers between devices, on_device(): sent.append(lax.ppermute(out, 'fsdp', ring_perm(slot == 5)))  47.7 us
    pallas_call x6, Pallas kernels, on_device(): call(functools.partial(hop_kernel, len(after)), message, 'hop%d' % slot,...  9.78 us
    pallas_call x1, Pallas kernels, on_device(): call(update_kernel, jax.ShapeDtypeStruct((ROWS, COLS), F32), 'update', (2...  6.86 us
    ppermute x4, starting transfers between devices, on_device(): lax.ppermute(x, 'fsdp', [(i, i ^ 1) for i in range(2 * CHIPS)])  5.46 us
    unnamed x24, local copies, waits for them, and re-layouts  5.16 us
    pallas_call x4, Pallas kernels, copied(): call(functools.partial(later_copy_kernel, SLOTS[begin:end]) if begin else...  5.09 us
    ppermute x7, starting transfers between devices, on_device(): sent.append(lax.ppermute(out, 'fsdp', ring_perm(slot == 5)))  4.59 us
    ppermute x3, starting transfers between devices, on_device(): lax.ppermute(kept, 'rep', rep_perm(dx, 0))  4.52 us
  transfers between devices with their start and end apart: 17, of which 12 were waited for; matrix products, arithmetic and copies ran while one was open for 0% of the time, Pallas kernels for 21%

profile of v1, /device:TPU:24, one launch (start us, length us, event | category | flops | bytes accessed | tf_op | source)
XLA Modules:
  0.0 110.1 jit_solution(11908508151431306907)
XLA Ops:
  0.6 3.1 %copy-done = bf16[128,28672]{1,0:T(8,128)(2,1)S(1)} copy-done((bf16[128,28672]{1,0:T(8,128)(2,1)S(1)}, bf16[128,28672]{1,0:T(8,128)(2,1)}, u32[]{:S(2)}) %copy-start) | copy-done | bytes 7340056
  7.8 2.0 %collective-permute-start.2 = (s16[3600,128]{1,0:T(8,128)(2,1)S(1)}, s16[3600,128]{1,0:T(8,128)(2,1)S(1)}, u32[]{:S(2)}, u32[]{:S(2)}) collective-permute-start(s16[3600,128]{1,0:T(8,128)(2,1)S(1)} %get-tuple-element.21.refs_0_.after), channel_id=1, source_target_pairs={{0,32},{16,240},{32,64},{48,16},{64,96},{80,48},{96,128},{112,80},... | collective-permute-start | bytes 2764808 | tf_op jit(solution)/shard_map/ppermute | solution.py:416
  10.6 2.0 %collective-permute-start.4 = (s16[3600,128]{1,0:T(8,128)(2,1)S(1)}, s16[3600,128]{1,0:T(8,128)(2,1)}, u32[]{:S(2)}, u32[]{:S(2)}) collective-permute-start(s16[3600,128]{1,0:T(8,128)(2,1)S(1)} %hop1.1.refs_0_), channel_id=1, source_target_pairs={{0,32},{16,240},{32,64},{48,16},{64,96},{80,48},{96,128},{112,80},... | collective-permute-start | bytes 2764808 | tf_op jit(solution)/shard_map/ppermute | solution.py:416
  14.3 2.9 %collective-permute-start.3 = (bf16[128,3584]{1,0:T(8,128)(2,1)}, bf16[128,3584]{1,0:T(8,128)(2,1)}, u32[]{:S(2)}, u32[]{:S(2)}) collective-permute-start(bf16[128,3584]{1,0:T(8,128)(2,1)} %get-tuple-element.25), channel_id=1, source_target_pairs={{0,16},{16,0},{32,48},{48,32},{64,80},{80,64},{96,112},{112,96},{1... | collective-permute-start | bytes 2752520 | tf_op jit(solution)/shard_map/ppermute | solution.py:316
  17.1 8.0 %collective-permute-done.2.refs_4_ = s16[3600,128]{1,0:T(8,128)(2,1)S(1)} collective-permute-done((s16[3600,128]{1,0:T(8,128)(2,1)S(1)}, s16[3600,128]{1,0:T(8,128)(2,1)S(1)}, u32[]{:S(2)}, u32[]{:S(2)}) %collective-permute-start.2) | collective-permute-done | bytes 921632 | tf_op jit(solution)/shard_map/ppermute | solution.py:416
  26.1 2.2 %copy567.1 = (bf16[128,5376]{1,0:T(8,128)(2,1)}, bf16[128,5376]{1,0:T(8,128)(2,1)S(1)}) custom-call(bf16[128,28672]{1,0:T(8,128)(2,1)S(1)} %bitcast.9, s16[3600,128]{1,0:T(8,128)(2,1)S(1)} %hop2.1.refs_0_.after), custom_call_target="tpu_custom_call" | custom-call | flops 235000000 | bytes 1400000 | tf_op jit(solution)/shard_map/copy567/pallas_call | solution.py:322
  28.4 2.0 %collective-permute-start.6 = (bf16[128,5376]{1,0:T(8,128)(2,1)}, bf16[128,5376]{1,0:T(8,128)(2,1)}, u32[]{:S(2)}, u32[]{:S(2)}) collective-permute-start(bf16[128,5376]{1,0:T(8,128)(2,1)} %get-tuple-element.28), channel_id=1, source_target_pairs={{0,16},{16,0},{32,48},{48,32},{64,80},{80,64},{96,112},{112,96},{1... | collective-permute-start | bytes 4128776 | tf_op jit(solution)/shard_map/ppermute | solution.py:316
  30.4 4.7 %collective-permute-done.4.refs_4_ = s16[3600,128]{1,0:T(8,128)(2,1)} collective-permute-done((s16[3600,128]{1,0:T(8,128)(2,1)S(1)}, s16[3600,128]{1,0:T(8,128)(2,1)}, u32[]{:S(2)}, u32[]{:S(2)}) %collective-permute-start.4) | collective-permute-done | bytes 921632 | tf_op jit(solution)/shard_map/ppermute | solution.py:416
  36.3 2.2 %hop3.1.refs_0_.after = s16[3600,128]{1,0:T(8,128)(2,1)S(1)} custom-call(s16[3600,128]{1,0:T(8,128)(2,1)S(1)} %hop2.1.refs_0_.after, bf16[256,256]{1,0:T(8,128)(2,1)S(1)} %get-tuple-element.22.refs_1_.refs_2_.in_t, bf16[128,3584]{1,0:T(8,128)(2,1)S(1)} %copy-done.2, bf16[128,3584]{1,0:T(8,128)(2,1)} %collective-permute-done.3.refs_3_.refs_4_, ...), custom_call_target="tpu_custom_call" | custom-call | flops 235000000 | bytes 1400000 | tf_op jit(solution)/shard_map/hop3/pallas_call | solution.py:404
  38.6 1.9 %tables.1 = (bf16[3584,256]{1,0:T(8,128)(2,1)S(1)}, f32[896,256]{1,0:T(8,128)S(1)}, f32[28,128]{1,0:T(8,128)S(1)}, f32[28,128]{1,0:T(8,128)S(1)}) custom-call(s32[28,4,32]{2,1,0:T(4,128)S(1)} %bitcast.12, s32[28,4]{1,0:T(8,128)S(1)} %copy.10.counts, f32[64,64]{1,0:T(8,128)S(1)} %copy-done.8, s16[3600,128]{1,0:T(8,128)(2,1)S(1)} %hop2.1.refs_0_.after), custom_call_target="tpu_custom_call" | custom-call | flops 235000000 | bytes 1400000 | tf_op jit(solution)/shard_map/tables/pallas_call | solution.py:352
  40.5 4.5 %collective-permute-done.5.refs_5_ = s16[3600,128]{1,0:T(8,128)(2,1)} collective-permute-done((s16[3600,128]{1,0:T(8,128)(2,1)S(1)}, s16[3600,128]{1,0:T(8,128)(2,1)}, u32[]{:S(2)}, u32[]{:S(2)}) %collective-permute-start.5) | collective-permute-done | bytes 921632 | tf_op jit(solution)/shard_map/ppermute | solution.py:416
  45.0 2.3 %hop4.1.refs_0_ = s16[3600,128]{1,0:T(8,128)(2,1)S(1)} custom-call(s16[3600,128]{1,0:T(8,128)(2,1)S(1)} %hop3.1.refs_0_.after, bf16[3584,256]{1,0:T(8,128)(2,1)S(1)} %get-tuple-element.26.refs_1_.basis, bf16[256,256]{1,0:T(8,128)(2,1)S(1)} %get-tuple-element.22.refs_1_.refs_2_.in_t, bf16[128,3584]{1,0:T(8,128)(2,1)S(1)} %copy-done.2, ...), custom_call_target="tpu_custom_call" | custom-call | flops 235000000 | bytes 1400000 | tf_op jit(solution)/shard_map/hop4/pallas_call | solution.py:404
  48.3 6.4 %collective-permute-done.7.refs_5_ = s16[3600,128]{1,0:T(8,128)(2,1)S(1)} collective-permute-done((s16[3600,128]{1,0:T(8,128)(2,1)S(1)}, s16[3600,128]{1,0:T(8,128)(2,1)S(1)}, u32[]{:S(2)}, u32[]{:S(2)}) %collective-permute-start.7) | collective-permute-done | bytes 921632 | tf_op jit(solution)/shard_map/ppermute | solution.py:416
  54.8 1.9 %hop5.1.refs_0_ = s16[3600,128]{1,0:T(8,128)(2,1)S(1)} custom-call(s16[3600,128]{1,0:T(8,128)(2,1)S(1)} %hop4.1.refs_0_, f32[256,1792]{1,0:T(8,128)S(1)} %momentum.1.refs_1_.mom_t, bf16[256,256]{1,0:T(8,128)(2,1)S(1)} %get-tuple-element.22.refs_1_.refs_2_.in_t, bf16[128,5376]{1,0:T(8,128)(2,1)S(1)} %get-tuple-element.27.refs_3_.refs_2_.own, ...), custom_call_target="tpu_custom_call" | custom-call | flops 235000000 | bytes 1400000 | tf_op jit(solution)/shard_map/hop5/pallas_call | solution.py:404
  56.8 7.9 %collective-permute-done.8.refs_4_ = s16[3600,128]{1,0:T(8,128)(2,1)S(1)} collective-permute-done((s16[3600,128]{1,0:T(8,128)(2,1)S(1)}, s16[3600,128]{1,0:T(8,128)(2,1)S(1)}, u32[]{:S(2)}, u32[]{:S(2)}) %collective-permute-start.8) | collective-permute-done | bytes 921632 | tf_op jit(solution)/shard_map/ppermute | solution.py:416
  64.6 1.9 %hop6.1 = s16[3600,128]{1,0:T(8,128)(2,1)S(1)} custom-call(s16[3600,128]{1,0:T(8,128)(2,1)S(1)} %hop5.1.refs_0_, bf16[256,256]{1,0:T(8,128)(2,1)S(1)} %get-tuple-element.22.refs_1_.refs_2_.in_t, bf16[128,5376]{1,0:T(8,128)(2,1)S(1)} %get-tuple-element.27.refs_3_.refs_2_.own, bf16[128,5376]{1,0:T(8,128)(2,1)} %collective-permute-done.6.refs_4_.refs_3_.sib, ...), custom_call_target="tpu_custom_call" | custom-call | flops 235000000 | bytes 1400000 | tf_op jit(solution)/shard_map/hop6/pallas_call | solution.py:404
  66.6 3.5 %collective-permute-done.10.msg = s16[3600,128]{1,0:T(8,128)(2,1)S(1)} collective-permute-done((s16[3600,128]{1,0:T(8,128)(2,1)S(1)}, s16[3600,128]{1,0:T(8,128)(2,1)S(1)}, u32[]{:S(2)}, u32[]{:S(2)}) %collective-permute-start.10) | collective-permute-done | bytes 921632 | tf_op jit(solution)/shard_map/ppermute | solution.py:416
  71.8 12.6 %collective-permute-done.9.msg = s16[3600,128]{1,0:T(8,128)(2,1)S(1)} collective-permute-done((s16[3600,128]{1,0:T(8,128)(2,1)S(1)}, s16[3600,128]{1,0:T(8,128)(2,1)S(1)}, u32[]{:S(2)}, u32[]{:S(2)}) %collective-permute-start.9) | collective-permute-done | bytes 921632 | tf_op jit(solution)/shard_map/ppermute | solution.py:416
  85.6 2.8 %collective-permute-start.13 = (f32[56,128]{1,0:T(8,128)S(1)}, f32[56,128]{1,0:T(8,128)S(1)}, u32[]{:S(2)}, u32[]{:S(2)}) collective-permute-start(f32[56,128]{1,0:T(8,128)S(1)} %get-tuple-element.33.kept), channel_id=1, source_target_pairs={{0,3},{1,0},{2,1},{3,2},{4,7},{5,4},{6,5},{7,6},{8,11},{9,8},{10,9... | collective-permute-start | bytes 86024 | tf_op jit(solution)/shard_map/ppermute | solution.py:446
  90.1 3.7 %collective-permute-done.12 = f32[56,128]{1,0:T(8,128)S(1)} collective-permute-done((f32[56,128]{1,0:T(8,128)S(1)}, f32[56,128]{1,0:T(8,128)S(1)}, u32[]{:S(2)}, u32[]{:S(2)}) %collective-permute-start.12) | collective-permute-done | bytes 28704 | tf_op jit(solution)/shard_map/ppermute | solution.py:446
  94.7 2.6 %collective-permute-start.15 = (f32[4,56,128]{2,1,0:T(8,128)S(1)}, f32[4,56,128]{2,1,0:T(8,128)S(1)}, u32[]{:S(2)}, u32[]{:S(2)}) collective-permute-start(f32[4,56,128]{2,1,0:T(8,128)S(1)} %pad_maximum_fusion.k0), channel_id=1, source_target_pairs={{0,8},{1,9},{2,10},{3,11},{4,12},{5,13},{6,14},{7,15},{8,0},{9,1},... | collective-permute-start | bytes 344072 | tf_op jit(solution)/shard_map/ppermute | solution.py:448
  97.3 3.1 %own.1 = f32[1792,256]{1,0:T(8,128)} custom-call(f32[256,1792]{1,0:T(8,128)S(1)} %get-tuple-element.32.updated, f32[56,128]{1,0:T(8,128)S(1)} %get-tuple-element.33.kept, bf16[3584,256]{1,0:T(8,128)(2,1)S(1)} %get-tuple-element.26.refs_1_.basis, f32[896,256]{1,0:T(8,128)S(1)} %get-tuple-element.29.cw), custom_call_target="tpu_custom_call" | custom-call | flops 235000000 | bytes 1400000 | tf_op jit(solution)/shard_map/own/pallas_call | solution.py:450
  101.0 2.3 %collective-permute-done.16.k3 = f32[4,56,128]{2,1,0:T(8,128)S(1)} collective-permute-done((f32[4,56,128]{2,1,0:T(8,128)S(1)}, f32[4,56,128]{2,1,0:T(8,128)S(1)}, u32[]{:S(2)}, u32[]{:S(2)}) %collective-permute-start.16) | collective-permute-done | bytes 114720 | tf_op jit(solution)/shard_map/ppermute | solution.py:448
  103.3 6.9 %update.1 = f32[1792,256]{1,0:T(8,128)} custom-call(f32[4,56,128]{2,1,0:T(8,128)S(1)} %pad_maximum_fusion.k0, f32[4,56,128]{2,1,0:T(8,128)S(1)} %collective-permute-done.14.k1, f32[4,56,128]{2,1,0:T(8,128)S(1)} %collective-permute-done.15.k2, f32[4,56,128]{2,1,0:T(8,128)S(1)} %collective-permute-done.16.k3, bf16[64,192]{1,0:T(8,128)(2,1)S(1)} %copy-done.7, ...), custom_call_target="tpu_custom_call" | custom-call | flops 235000000 | bytes 1400000 | tf_op jit(solution)/shard_map/update/pallas_call | solution.py:464
  (54 shorter events, 16.0 us)
Async XLA Ops:
  0.6 3.1 %copy-start = (bf16[128,28672]{1,0:T(8,128)(2,1)S(1)}, bf16[128,28672]{1,0:T(8,128)(2,1)}, u32[]{:S(2)}) copy-start(bf16[128,28672]{1,0:T(8,128)(2,1)} %cot.7) | copy-start | bytes 22020100
  4.6 8.0 %slice-start = ((s8[7340032]{0:T(1024)(128)(4,1)}), s8[4194304]{0:T(1024)(128)(4,1)S(1)}, s32[]{:S(2)}) async-start(s8[7340032]{0:T(1024)(128)(4,1)} %bitcast.8), calls=%async_computation | async-start | bytes 8388608
  5.0 7.6 %slice-start.1 = ((s8[7340032]{0:T(1024)(128)(4,1)}), s8[3145728]{0:T(1024)(128)(4,1)S(1)}, s32[]{:S(2)}) async-start(s8[7340032]{0:T(1024)(128)(4,1)} %bitcast.8), calls=%async_computation.1 | async-start | bytes 6291456
  5.0 2.0 %collective-permute-start = (bf16[128,2048]{1,0:T(8,128)(2,1)S(1)}, bf16[128,2048]{1,0:T(8,128)(2,1)S(1)}, u32[]{:S(2)}, u32[]{:S(2)}) collective-permute-start(bf16[128,2048]{1,0:T(8,128)(2,1)S(1)} %get-tuple-element.18.after), channel_id=1, source_target_pairs={{0,16},{16,0},{32,48},{48,32},{64,80},{80,64},{96,112},{112,96},{1... | collective-permute-start | bytes 1572872 | tf_op jit(solution)/shard_map/ppermute | solution.py:316
  5.9 3.9 %collective-permute-start.1 = (bf16[128,3584]{1,0:T(8,128)(2,1)S(1)}, bf16[128,3584]{1,0:T(8,128)(2,1)S(1)}, u32[]{:S(2)}, u32[]{:S(2)}) collective-permute-start(bf16[128,3584]{1,0:T(8,128)(2,1)S(1)} %get-tuple-element.20.after), channel_id=1, source_target_pairs={{0,16},{16,0},{32,48},{48,32},{64,80},{80,64},{96,112},{112,96},{1... | collective-permute-start | bytes 2752520 | tf_op jit(solution)/shard_map/ppermute | solution.py:316
  7.8 17.3 %collective-permute-start.2 = (s16[3600,128]{1,0:T(8,128)(2,1)S(1)}, s16[3600,128]{1,0:T(8,128)(2,1)S(1)}, u32[]{:S(2)}, u32[]{:S(2)}) collective-permute-start(s16[3600,128]{1,0:T(8,128)(2,1)S(1)} %get-tuple-element.21.refs_0_.after), channel_id=1, source_target_pairs={{0,32},{16,240},{32,64},{48,16},{64,96},{80,48},{96,128},{112,80},... | collective-permute-start | bytes 2764808 | tf_op jit(solution)/shard_map/ppermute | solution.py:416
  10.6 24.6 %collective-permute-start.4 = (s16[3600,128]{1,0:T(8,128)(2,1)S(1)}, s16[3600,128]{1,0:T(8,128)(2,1)}, u32[]{:S(2)}, u32[]{:S(2)}) collective-permute-start(s16[3600,128]{1,0:T(8,128)(2,1)S(1)} %hop1.1.refs_0_), channel_id=1, source_target_pairs={{0,32},{16,240},{32,64},{48,16},{64,96},{80,48},{96,128},{112,80},... | collective-permute-start | bytes 2764808 | tf_op jit(solution)/shard_map/ppermute | solution.py:416
  14.3 11.7 %copy-start.1 = (bf16[128,3584]{1,0:T(8,128)(2,1)}, bf16[128,3584]{1,0:T(8,128)(2,1)S(1)}, u32[]{:S(2)}) copy-start(bf16[128,3584]{1,0:T(8,128)(2,1)S(1)} %get-tuple-element.24.refs_2_.refs_3_) | copy-start | bytes 2752516
  14.3 16.2 %collective-permute-start.3 = (bf16[128,3584]{1,0:T(8,128)(2,1)}, bf16[128,3584]{1,0:T(8,128)(2,1)}, u32[]{:S(2)}, u32[]{:S(2)}) collective-permute-start(bf16[128,3584]{1,0:T(8,128)(2,1)} %get-tuple-element.25), channel_id=1, source_target_pairs={{0,16},{16,0},{32,48},{48,32},{64,80},{80,64},{96,112},{112,96},{1... | collective-permute-start | bytes 2752520 | tf_op jit(solution)/shard_map/ppermute | solution.py:316
  26.0 4.3 %copy-start.9 = (s32[1,28,4]{1,2,0:T(4,128)S(1)}, s32[1,28,4]{1,2,0:T(4,128)}, u32[]{:S(2)}) copy-start(s32[1,28,4]{1,2,0:T(4,128)} %param.12) | copy-start | bytes 1348
  26.0 19.0 %collective-permute-start.5 = (s16[3600,128]{1,0:T(8,128)(2,1)S(1)}, s16[3600,128]{1,0:T(8,128)(2,1)}, u32[]{:S(2)}, u32[]{:S(2)}) collective-permute-start(s16[3600,128]{1,0:T(8,128)(2,1)S(1)} %hop2.1.refs_0_.after), channel_id=1, source_target_pairs={{0,32},{16,240},{32,64},{48,16},{64,96},{80,48},{96,128},{112,80},... | collective-permute-start | bytes 2764808 | tf_op jit(solution)/shard_map/ppermute | solution.py:416
  28.4 26.4 %collective-permute-start.6 = (bf16[128,5376]{1,0:T(8,128)(2,1)}, bf16[128,5376]{1,0:T(8,128)(2,1)}, u32[]{:S(2)}, u32[]{:S(2)}) collective-permute-start(bf16[128,5376]{1,0:T(8,128)(2,1)} %get-tuple-element.28), channel_id=1, source_target_pairs={{0,16},{16,0},{32,48},{48,32},{64,80},{80,64},{96,112},{112,96},{1... | collective-permute-start | bytes 4128776 | tf_op jit(solution)/shard_map/ppermute | solution.py:316
  38.5 16.3 %collective-permute-start.7 = (s16[3600,128]{1,0:T(8,128)(2,1)S(1)}, s16[3600,128]{1,0:T(8,128)(2,1)S(1)}, u32[]{:S(2)}, u32[]{:S(2)}) collective-permute-start(s16[3600,128]{1,0:T(8,128)(2,1)S(1)} %hop3.1.refs_0_.after), channel_id=1, source_target_pairs={{0,32},{16,240},{32,64},{48,16},{64,96},{80,48},{96,128},{112,80},... | collective-permute-start | bytes 2764808 | tf_op jit(solution)/shard_map/ppermute | solution.py:416
  47.3 17.3 %collective-permute-start.8 = (s16[3600,128]{1,0:T(8,128)(2,1)S(1)}, s16[3600,128]{1,0:T(8,128)(2,1)S(1)}, u32[]{:S(2)}, u32[]{:S(2)}) collective-permute-start(s16[3600,128]{1,0:T(8,128)(2,1)S(1)} %hop4.1.refs_0_), channel_id=1, source_target_pairs={{0,32},{16,240},{32,64},{48,16},{64,96},{80,48},{96,128},{112,80},... | collective-permute-start | bytes 2764808 | tf_op jit(solution)/shard_map/ppermute | solution.py:416
  56.7 13.5 %collective-permute-start.10 = (s16[3600,128]{1,0:T(8,128)(2,1)S(1)}, s16[3600,128]{1,0:T(8,128)(2,1)S(1)}, u32[]{:S(2)}, u32[]{:S(2)}) collective-permute-start(s16[3600,128]{1,0:T(8,128)(2,1)S(1)} %hop5.1.refs_0_), channel_id=1, source_target_pairs={{0,48},{16,224},{32,80},{48,0},{64,112},{80,32},{96,144},{112,64},... | collective-permute-start | bytes 2764808 | tf_op jit(solution)/shard_map/ppermute | solution.py:416
  66.5 17.9 %collective-permute-start.9 = (s16[3600,128]{1,0:T(8,128)(2,1)S(1)}, s16[3600,128]{1,0:T(8,128)(2,1)S(1)}, u32[]{:S(2)}, u32[]{:S(2)}) collective-permute-start(s16[3600,128]{1,0:T(8,128)(2,1)S(1)} %hop6.1), channel_id=1, source_target_pairs={{0,32},{16,240},{32,64},{48,16},{64,96},{80,48},{96,128},{112,80},... | collective-permute-start | bytes 2764808 | tf_op jit(solution)/shard_map/ppermute | solution.py:416
  85.6 4.5 %collective-permute-start.13 = (f32[56,128]{1,0:T(8,128)S(1)}, f32[56,128]{1,0:T(8,128)S(1)}, u32[]{:S(2)}, u32[]{:S(2)}) collective-permute-start(f32[56,128]{1,0:T(8,128)S(1)} %get-tuple-element.33.kept), channel_id=1, source_target_pairs={{0,3},{1,0},{2,1},{3,2},{4,7},{5,4},{6,5},{7,6},{8,11},{9,8},{10,9... | collective-permute-start | bytes 86024 | tf_op jit(solution)/shard_map/ppermute | solution.py:446
  88.5 5.4 %collective-permute-start.12 = (f32[56,128]{1,0:T(8,128)S(1)}, f32[56,128]{1,0:T(8,128)S(1)}, u32[]{:S(2)}, u32[]{:S(2)}) collective-permute-start(f32[56,128]{1,0:T(8,128)S(1)} %get-tuple-element.33.kept), channel_id=1, source_target_pairs={{0,2},{1,3},{2,0},{3,1},{4,6},{5,7},{6,4},{7,5},{8,10},{9,11},{10,... | collective-permute-start | bytes 86024 | tf_op jit(solution)/shard_map/ppermute | solution.py:446
  89.3 5.1 %collective-permute-start.11 = (f32[56,128]{1,0:T(8,128)S(1)}, f32[56,128]{1,0:T(8,128)S(1)}, u32[]{:S(2)}, u32[]{:S(2)}) collective-permute-start(f32[56,128]{1,0:T(8,128)S(1)} %get-tuple-element.33.kept), channel_id=1, source_target_pairs={{0,1},{1,2},{2,3},{3,0},{4,5},{5,6},{6,7},{7,4},{8,9},{9,10},{10,1... | collective-permute-start | bytes 86024 | tf_op jit(solution)/shard_map/ppermute | solution.py:446
  94.4 6.0 %collective-permute-start.14 = (f32[4,56,128]{2,1,0:T(8,128)S(1)}, f32[4,56,128]{2,1,0:T(8,128)S(1)}, u32[]{:S(2)}, u32[]{:S(2)}) collective-permute-start(f32[4,56,128]{2,1,0:T(8,128)S(1)} %pad_maximum_fusion.k0), channel_id=1, source_target_pairs={{0,4},{1,5},{2,6},{3,7},{4,8},{5,9},{6,10},{7,11},{8,12},{9,13},{1... | collective-permute-start | bytes 344072 | tf_op jit(solution)/shard_map/ppermute | solution.py:448
  94.7 6.3 %collective-permute-start.15 = (f32[4,56,128]{2,1,0:T(8,128)S(1)}, f32[4,56,128]{2,1,0:T(8,128)S(1)}, u32[]{:S(2)}, u32[]{:S(2)}) collective-permute-start(f32[4,56,128]{2,1,0:T(8,128)S(1)} %pad_maximum_fusion.k0), channel_id=1, source_target_pairs={{0,8},{1,9},{2,10},{3,11},{4,12},{5,13},{6,14},{7,15},{8,0},{9,1},... | collective-permute-start | bytes 344072 | tf_op jit(solution)/shard_map/ppermute | solution.py:448
  97.2 6.0 %collective-permute-start.16 = (f32[4,56,128]{2,1,0:T(8,128)S(1)}, f32[4,56,128]{2,1,0:T(8,128)S(1)}, u32[]{:S(2)}, u32[]{:S(2)}) collective-permute-start(f32[4,56,128]{2,1,0:T(8,128)S(1)} %pad_maximum_fusion.k0), channel_id=1, source_target_pairs={{0,12},{1,13},{2,14},{3,15},{4,0},{5,1},{6,2},{7,3},{8,4},{9,5},{1... | collective-permute-start | bytes 344072 | tf_op jit(solution)/shard_map/ppermute | solution.py:448
  97.2 6.0 %copy-start.4 = (bf16[768,256]{1,0:T(8,128)(2,1)S(1)}, bf16[768,256]{1,0:T(8,128)(2,1)}, u32[]{:S(2)}) copy-start(bf16[768,256]{1,0:T(8,128)(2,1)} %constant.8.clone.cos4_3) | copy-start | bytes 1179652
  97.3 6.0 %copy-start.7 = (bf16[64,192]{1,0:T(8,128)(2,1)S(1)}, bf16[64,192]{1,0:T(8,128)(2,1)}, u32[]{:S(2)}) copy-start(bf16[64,192]{1,0:T(8,128)(2,1)} %constant.7.clone.cos_t3) | copy-start | bytes 73732
  (5 other events, 9.2 us)

commit v2 on v1

--- a/solution.py
+++ b/solution.py
@@ -21,7 +21,6 @@
 HALF_GROUPS = GROUPS // 2
 GROUPS = ROWS // GROUP
 HALF_GROUPS = GROUPS // 2
-MSG = TILES * COLS + 16
 N_REP = 16
 STEP = 64.0
 TOP = 32760.0
@@ -38,6 +37,7 @@
     (1, False),
     (0, False),
 )
+PARTS = (1, 1, 1, 1, 1, 1, 1)
 VMEM_LIMIT = 24 * 1024 * 1024
 
 
@@ -78,13 +78,23 @@
     return high, (x - high.astype(F32)).astype(BF16)
 
 
-def read_scales(msg):
-    codes = msg[TILES * COLS : MSG, :].astype(F32)
-    return jnp.exp2(codes * (1.0 / STEP)) * (1.0 / TOP)
-
-
-def read_tile(msg, scales, j):
-    return msg[j * COLS : (j + 1) * COLS, :].astype(F32) * scales[j : j + 1, :]
+def part_rows(parts):
+    return TILES // parts * COLS + 16
+
+
+def read_message(parts):
+    count = TILES // len(parts)
+    scales = []
+    for msg in parts:
+        codes = msg[count * COLS :, :].astype(F32)
+        scales.append(jnp.exp2(codes * (1.0 / STEP)) * (1.0 / TOP))
+
+    def tile(j):
+        n, j = j // count, j % count
+        rows = parts[n][j * COLS : (j + 1) * COLS, :]
+        return rows.astype(F32) * scales[n][j : j + 1, :]
+
+    return tile
 
 
 def partial_tile(in_t, own, sib, j):
@@ -93,24 +103,27 @@
     return jnp.dot(in_t, tokens, preferred_element_type=F32)
 
 
-def write_message(out, tiles):
-    codes = []
-    for j, tile in enumerate(tiles):
-        top = jnp.maximum(jnp.max(jnp.abs(tile), axis=0, keepdims=True), 1e-30)
-        code = jnp.ceil(jnp.log2(top) * STEP)
-        inv = jnp.exp2(code * (-1.0 / STEP)) * TOP
-        out[j * COLS : (j + 1) * COLS, :] = jnp.round(tile * inv).astype(jnp.int32).astype(jnp.int16)
-        codes.append(code)
-    codes.append(jnp.zeros((16 - len(codes), 128), F32))
-    out[TILES * COLS : MSG, :] = jnp.concatenate(codes, axis=0).astype(jnp.int32).astype(jnp.int16)
-
-
-def copy_kernel(slots, cot, extra, send, own, sems):
+def write_message(parts, tiles):
+    count = TILES // len(parts)
+    for n, out in enumerate(parts):
+        codes = []
+        for j, tile in enumerate(tiles[n * count : (n + 1) * count]):
+            top = jnp.maximum(jnp.max(jnp.abs(tile), axis=0, keepdims=True), 1e-30)
+            code = jnp.ceil(jnp.log2(top) * STEP)
+            scaled = jnp.round(tile * (jnp.exp2(code * (-1.0 / STEP)) * TOP))
+            out[j * COLS : (j + 1) * COLS, :] = scaled.astype(jnp.int32).astype(jnp.int16)
+            codes.append(code)
+        codes.append(jnp.zeros((16 - count, 128), F32))
+        codes = jnp.concatenate(codes, axis=0)
+        out[count * COLS :, :] = codes.astype(jnp.int32).astype(jnp.int16)
+
+
+def copy_kernel(slots, cot, after, send, own, sems):
     place = lax.axis_index("fsdp")
     chip, core = place // 2, place % 2
     copies = []
     for whose, out in ((1 - core, send), (core, own)):
-        for n, (k, flip) in enumerate(slots if out is not None else ()):
+        for n, (k, flip) in enumerate(slots):
             to = (chip + k * (1 - 2 * whose) + CHIPS) % CHIPS
             start = pl.multiple_of((2 * to + (1 - whose if flip else whose)) * ROWS, 128)
             for row in range(0, TOK, 32):
@@ -125,35 +138,26 @@
     copies = [pltpu.make_async_copy(*c) for c in copies]
     for c in copies:
         c.start()
-    if extra is not None:
-        send[:, len(slots) * ROWS :] = extra[...]
     for c in copies:
         c.wait()
 
 
-def first_copy_kernel(cot, extra, send, own, sems):
-    copy_kernel(SLOTS[:1], cot, extra, send, own, sems)
-
-
-def later_copy_kernel(slots, cot, after, send, own, sems):
-    copy_kernel(slots, cot, None, send, own, sems)
-
-
-def first_hop_kernel(in_own, in_sib, own, sib, after, in_t, out):
+def first_hop_kernel(in_own, in_sib, own, sib, after, in_t, *outs):
     in_t[:, :TOK] = in_own[...].astype(F32).T.astype(BF16)
     in_t[:, TOK:] = in_sib[...].astype(F32).T.astype(BF16)
     both = in_t[...]
-    write_message(out, [partial_tile(both, own, sib, j) for j in range(TILES)])
-
-
-def hop_kernel(n_after, *refs):
-    in_t, own, sib, *recv, out = refs[n_after:]
+    write_message(outs, [partial_tile(both, own, sib, j) for j in range(TILES)])
+
+
+def hop_kernel(n_after, n_recv, *refs):
+    in_t, own, sib, *refs = refs[n_after:]
+    recv, outs = refs[:n_recv], refs[n_recv:]
     both = in_t[...]
     tiles = [partial_tile(both, own, sib, j) for j in range(TILES)]
     if recv:
-        scales = read_scales(recv[0])
-        tiles = [tile + read_tile(recv[0], scales, j) for j, tile in enumerate(tiles)]
-    write_message(out, tiles)
+        read = read_message(recv)
+        tiles = [tile + read(j) for j, tile in enumerate(tiles)]
+    write_message(outs, tiles)
 
 
 def tables_kernel(listed, counts, cos_t, after, basis, cw, valid, places):
@@ -196,21 +200,22 @@
     return out
 
 
-def base_kernel(in_t, own, sib, msg, mom_t, out):
+def base_kernel(after1, after2, after3, in_t, own, sib, mom_t, *refs):
     both = in_t[...]
-    scales = read_scales(msg)
+    out = refs[-1]
+    read = read_message(refs[:-1])
     for j in range(TILES):
         cols = slice(j * 128, (j + 1) * 128)
-        out[:, cols] = partial_tile(both, own, sib, j) + mom_t[:, cols] + read_tile(msg, scales, j)
-
-
-def kept_kernel(msg, base, basis, cw, valid, places, updated, kept):
-    kept[GROUPS:, :] = places[...]
+        out[:, cols] = partial_tile(both, own, sib, j) + mom_t[:, cols] + read(j)
+
+
+def kept_kernel(base, basis, cw, valid, *refs):
+    updated, kept = refs[-2:]
+    read = read_message(refs[:-2])
     column = (lax.broadcasted_iota(jnp.int32, (GROUP, 256), 1) & 127) >> 5
-    scales = read_scales(msg)
     for p in range(TILES):
         cols = slice(p * 128, (p + 1) * 128)
-        tile = base[:, cols] + read_tile(msg, scales, p)
+        tile = base[:, cols] + read(p)
         updated[:, cols] = tile
         high, low = split(tile)
         b_high = basis[p * 256 : p * 256 + 128, :]
@@ -230,7 +235,8 @@
             kept[at, :] = jnp.where(valid[at, :] > 0.0, half, 0.0)
 
 
-def own_kernel(updated, kept, basis, cw, out):
+def own_kernel(updated, kept, basis, cw, out, done):
+    done[...] = jnp.zeros(done.shape, F32)
     g = pl.program_id(0)
     column = (lax.broadcasted_iota(jnp.int32, (GROUP, 256), 1) & 127) >> 5
     for p in range(TILES // 2):
@@ -252,25 +258,22 @@
         out[cols, :] = (updated[:, cols] - decoded).T
 
 
-def update_kernel(k0, k1, k2, k3, cos_t3, cos4_3, out, kept, index):
+def arrange_kernel(k0, k1, k2, k3, after, out):
+    for j, rows in enumerate(by_column_group([k0[...], k1[...], k2[...], k3[...]])):
+        out[j] = rows
+
+
+def update_kernel(k0, k1, k2, k3, n0, n1, n2, n3, cos_t3, cos4_3, out):
     g = pl.program_id(0)
-
-    @pl.when(g == 0)
-    def _():
-        for y, ref in enumerate((k0, k1, k2, k3)):
-            for rows, arranged in ((slice(0, GROUPS), kept), (slice(GROUPS, 2 * GROUPS), index)):
-                groups = by_column_group([ref[x, rows, :] for x in range(4)])
-                for j in range(4):
-                    arranged[j, y] = groups[j]
-
     row = lax.broadcasted_iota(jnp.int32, (GROUP, 512), 0).astype(F32).astype(BF16)
     one, zero = jnp.ones((GROUP, 512), BF16), jnp.zeros((GROUP, 512), BF16)
     dense = []
     for i in range(HALF_GROUPS):
         at = pl.ds(g * HALF_GROUPS + i, 1)
         for j in range(4):
-            k = jnp.concatenate([kept[j, y, at, :] for y in range(4)], axis=1)
-            n = jnp.concatenate([index[j, y, at, :] for y in range(4)], axis=1).astype(jnp.int32)
+            k = jnp.concatenate([ref[j, at, :] for ref in (k0, k1, k2, k3)], axis=1)
+            n = jnp.concatenate([ref[j, at, :] for ref in (n0, n1, n2, n3)], axis=1)
+            n = n.astype(jnp.int32)
             high, low = split(k)
             here = row == (n >> 6).astype(F32).astype(BF16)
             left = jnp.concatenate(
@@ -316,28 +319,36 @@
     swap = lambda x: lax.ppermute(x, "fsdp", [(i, i ^ 1) for i in range(2 * CHIPS)])
     own_of, theirs_of = [], []
 
-    def copied(begin, end, after, name):
-        n = end - begin
-        extra = COLS if begin == 0 else 0
-        send, own = call(
-            functools.partial(later_copy_kernel, SLOTS[begin:end]) if begin else first_copy_kernel,
-            (
-                jax.ShapeDtypeStruct((TOK, n * ROWS + extra), BF16),
-                jax.ShapeDtypeStruct((TOK, n * ROWS), BF16),
-            ),
-            name,
-            (1,),
-            [AFTER, AFTER if begin else whole(TOK, COLS)],
-            (whole(TOK, n * ROWS + extra), whole(TOK, n * ROWS)),
-            scratch=[pltpu.SemaphoreType.DMA((8 * n,))],
-        )(cotangent, after)
+    def exchanged(send, own, n):
         theirs = swap(send)
         own_of.extend((own, i) for i in range(n))
         theirs_of.extend((theirs, i) for i in range(n))
-        return send, theirs
-
-    first, first_theirs = copied(0, 1, inputs, "copy0")
-    second, _ = copied(1, 3, first, "copy12")
+        return theirs
+
+    def copied(begin, end, after, name):
+        n = end - begin
+        shape = jax.ShapeDtypeStruct((TOK, n * ROWS), BF16)
+        send, own = call(
+            functools.partial(copy_kernel, SLOTS[begin:end]),
+            (shape, shape),
+            name,
+            (1,),
+            [AFTER, AFTER],
+            (whole(TOK, n * ROWS), whole(TOK, n * ROWS)),
+            scratch=[pltpu.SemaphoreType.DMA((8 * n,))],
+        )(cotangent, after)
+        exchanged(send, own, n)
+        return send
+
+    place = lax.axis_index("fsdp")
+    across = (place + CHIPS) % (2 * CHIPS)
+    first, first_own = (
+        lax.dynamic_slice(cotangent, (0, block * ROWS), (TOK, ROWS))
+        for block in (across ^ 1, across)
+    )
+    exchanged(first, first_own, 1)
+    in_sib = swap(inputs)
+    second = copied(1, 3, first, "copy12")
 
     def blocks(slot):
         specs, args = [], []
@@ -346,7 +357,12 @@
             args.append(array)
         return specs, args
 
-    message = jax.ShapeDtypeStruct((MSG, 128), jnp.int16)
+    def message(slot):
+        rows = part_rows(PARTS[slot])
+        return (
+            (jax.ShapeDtypeStruct((rows, 128), jnp.int16),) * PARTS[slot],
+            (whole(rows, 128),) * PARTS[slot],
+        )
 
     def made_tables(after):
         return call(
@@ -373,6 +389,22 @@
             pl.BlockSpec((COLS, HALF), lambda g: (0, g)),
         )(momentum, after)
 
+    def along_x(rows):
+        return [lax.ppermute(rows, "rep", rep_perm(dx, 0)) for dx in (1, 2, 3)]
+
+    def along_y(rows):
+        return [rows] + [lax.ppermute(rows, "rep", rep_perm(0, dy)) for dy in (1, 2, 3)]
+
+    def arranged(rows, from_x, after, name):
+        return call(
+            arrange_kernel,
+            jax.ShapeDtypeStruct((4, GROUPS, 128), F32),
+            name,
+            (1,),
+            [whole(GROUPS, 128)] * 4 + [AFTER],
+            whole(4, GROUPS, 128),
+        )(rows, *from_x, after)
+
     made, sent = [], []
     for slot in range(7):
         if slot == 1:
@@ -380,40 +412,45 @@
         if slot == 3:
             copied(5, 8, made[2], "copy567")
         specs, args = blocks(slot)
+        shapes, out_specs = message(slot)
         if slot == 0:
-            in_t, out = call(
+            in_t, *outs = call(
                 first_hop_kernel,
-                (jax.ShapeDtypeStruct((COLS, 2 * TOK), BF16), message),
+                (jax.ShapeDtypeStruct((COLS, 2 * TOK), BF16),) + shapes,
                 "hop0",
                 (1,),
-                [whole(TOK, COLS), pl.BlockSpec((TOK, COLS), lambda g: (0, ROWS // COLS))]
+                [whole(TOK, COLS), whole(TOK, COLS)]
                 + specs
                 + [AFTER],
-                (whole(COLS, 2 * TOK), whole(MSG, 128)),
-            )(inputs, first_theirs, *args, second)
+                (whole(COLS, 2 * TOK),) + out_specs,
+            )(inputs, in_sib, *args, second)
         else:
-            recv = sent[slot - 2 : slot - 1]
+            recv, recv_specs = ((), ()) if slot < 2 else (sent[slot - 2], message(slot - 2)[1])
             after = (made[-1],)
+            if slot == 2:
+                basis, cw, valid, places = made_tables(made[1])
+                places_x = along_x(places)
             if slot == 3:
-                basis, cw, valid, places = made_tables(made[2])
+                after = (made[-1], basis)
+                mom_t = momentum_t(momentum[0], made[2])
             if slot == 4:
-                after = (made[-1], basis)
-                mom_t = momentum_t(momentum[0], made[3])
+                after = (made[-1], mom_t)
+                places_all = along_y(arranged(places, places_x, made[3], "places"))
             if slot == 5:
-                after = (made[-1], mom_t)
-            out = call(
-                functools.partial(hop_kernel, len(after)),
-                message,
+                after = (made[-1], places_all[0])
+            outs = call(
+                functools.partial(hop_kernel, len(after), len(recv)),
+                shapes,
                 "hop%d" % slot,
                 (1,),
                 [AFTER] * len(after)
                 + [whole(COLS, 2 * TOK)]
                 + specs
-                + [whole(MSG, 128)] * len(recv),
-                whole(MSG, 128),
+                + list(recv_specs),
+                out_specs,
             )(*after, in_t, *args, *recv)
-        made.append(out)
-        sent.append(lax.ppermute(out, "fsdp", ring_perm(slot == 5)))
+        made.append(outs[-1])
+        sent.append([lax.ppermute(out, "fsdp", ring_perm(slot == 5)) for out in outs])
 
     specs, args = blocks(7)
     base = call(
@@ -421,55 +458,51 @@
         jax.ShapeDtypeStruct((COLS, ROWS), F32),
         "base",
         (1,),
-        [whole(COLS, 2 * TOK)] + specs + [whole(MSG, 128), whole(COLS, ROWS)],
+        [AFTER] * 3 + [whole(COLS, 2 * TOK)] + specs + [whole(COLS, ROWS)] + list(message(5)[1]),
         whole(COLS, ROWS),
-    )(in_t, *args, sent[5], mom_t)
+    )(*places_all[1:], in_t, *args, mom_t, *sent[5])
     updated, kept = call(
         kept_kernel,
         (
             jax.ShapeDtypeStruct((COLS, ROWS), F32),
-            jax.ShapeDtypeStruct((2 * GROUPS, 128), F32),
+            jax.ShapeDtypeStruct((GROUPS, 128), F32),
         ),
         "kept",
         (1,),
         [
-            whole(MSG, 128),
             whole(COLS, ROWS),
             whole(TILES * 256, 256),
             whole(TILES * GROUP, 256),
             whole(GROUPS, 128),
-            whole(GROUPS, 128),
-        ],
-        (whole(COLS, ROWS), whole(2 * GROUPS, 128)),
-    )(sent[6], base, basis, cw, valid, places)
-    along_x = jnp.stack(
-        [kept] + [lax.ppermute(kept, "rep", rep_perm(dx, 0)) for dx in (1, 2, 3)]
-    )
-    kept_all = [along_x] + [lax.ppermute(along_x, "rep", rep_perm(0, dy)) for dy in (1, 2, 3)]
-
-    new_momentum = call(
+        ]
+        + list(message(6)[1]),
+        (whole(COLS, ROWS), whole(GROUPS, 128)),
+    )(base, basis, cw, valid, *sent[6])
+    from_x = along_x(kept)
+    new_momentum, own_done = call(
         own_kernel,
-        jax.ShapeDtypeStruct((ROWS, COLS), F32),
+        (jax.ShapeDtypeStruct((ROWS, COLS), F32), jax.ShapeDtypeStruct((8, 128), F32)),
         "own",
         (2,),
         [
             pl.BlockSpec((COLS, HALF), lambda g: (0, g)),
-            whole(2 * GROUPS, 128),
+            whole(GROUPS, 128),
             pl.BlockSpec((TILES * 128, 256), lambda g: (g, 0)),
             pl.BlockSpec((TILES * GROUP // 2, 256), lambda g: (g, 0)),
         ],
-        pl.BlockSpec((HALF, COLS), lambda g: (g, 0)),
+        (pl.BlockSpec((HALF, COLS), lambda g: (g, 0)), whole(8, 128)),
     )(updated, kept, basis, cw)
+
+    kept_all = along_y(arranged(kept, from_x, own_done, "arrange"))
 
     update = call(
         update_kernel,
         jax.ShapeDtypeStruct((ROWS, COLS), F32),
         "update",
         (2,),
-        [whole(4, 2 * GROUPS, 128)] * 4 + [whole(GROUP, 3 * GROUP), whole(3 * COLS, COLS)],
+        [whole(4, GROUPS, 128)] * 8 + [whole(GROUP, 3 * GROUP), whole(3 * COLS, COLS)],
         pl.BlockSpec((HALF, COLS), lambda g: (g, 0)),
-        scratch=[pltpu.VMEM((4, 4, GROUPS, 128), F32)] * 2,
-    )(*kept_all, cos_t3, cos4_3)
+    )(*kept_all, *places_all, cos_t3, cos4_3)
     return new_momentum[None], update
 
 

time: 110 us -> 109 us (level)
  waiting for transfers between devices: 55.3 us -> 41.7 us
  starting transfers between devices: 17.5 us -> 30 us
    ppermute x13 -> x19, waiting for transfers between devices: 54.8 us -> 41.7 us  [the longest x7 30 us: on_device(): lax.ppermute(out, 'fsdp', ring_perm(slot == 5))]
    ppermute x13 -> x19, starting transfers between devices: 12 us -> 23.6 us  [the longest x6 11.6 us: along_x(): return [lax.ppermute(rows, 'rep', rep_perm(dx, 0)) for dx in (1, 2, 3)]]
    dynamic_slice x0 -> x1, local copies, waits for them, and re-layouts: none -> 1.22 us  [on_device(): lax.dynamic_slice(cotangent, (0, block * ROWS), (TOK, ROWS))]
    ppermute x4 -> x5, starting transfers between devices: 5.46 us -> 6.44 us  [on_device(): lax.ppermute(x, 'fsdp', [(i, i ^ 1) for i in range(2 * CHIPS)])]
    unnamed x24 -> x22, local copies, waits for them, and re-layouts: 5.16 us -> 4.33 us
    pallas_call x12 -> x13, Pallas kernels: 18.8 us -> 18.6 us  [the longest x6 9.87 us: on_device(): call(functools.partial(hop_kernel, len(after), len(recv)), shapes, 'hop%d...]
  transfers between devices with their start and end apart: 17 -> 24, of which waited for: 12 -> 13; matrix products, arithmetic and copies ran while one was open for 0% -> 0% of each run, Pallas kernels for 21% -> 21%
where the time goes in v2:
time: 109 us
  waiting for transfers between devices  41.7 us (38%)
  Pallas kernels  30.5 us (28%)
  starting transfers between devices  30 us (28%)
  local copies, waits for them, and re-layouts  5.65 us (5%)
    ppermute x7, waiting for transfers between devices, on_device(): lax.ppermute(out, 'fsdp', ring_perm(slot == 5))  30 us
    ppermute x6, starting transfers between devices, along_x(): return [lax.ppermute(rows, 'rep', rep_perm(dx, 0)) for dx in (1, 2, 3)]  11.6 us
    pallas_call x6, Pallas kernels, on_device(): call(functools.partial(hop_kernel, len(after), len(recv)), shapes, 'hop%d...  9.87 us
    ppermute x6, waiting for transfers between devices, along_y(): lax.ppermute(rows, 'rep', rep_perm(0, dy))  8.74 us
    ppermute x6, starting transfers between devices, along_y(): lax.ppermute(rows, 'rep', rep_perm(0, dy))  7.45 us
    ppermute x5, starting transfers between devices, on_device(): lax.ppermute(x, 'fsdp', [(i, i ^ 1) for i in range(2 * CHIPS)])  6.44 us
    pallas_call x1, Pallas kernels, on_device(): call(update_kernel, jax.ShapeDtypeStruct((ROWS, COLS), F32), 'update', (2...  6.37 us
    pallas_call x3, Pallas kernels, copied(): call(functools.partial(copy_kernel, SLOTS[begin:end]), (shape, shape), na...  4.67 us
  transfers between devices with their start and end apart: 24, of which 13 were waited for; matrix products, arithmetic and copies ran while one was open for 0% of the time, Pallas kernels for 21%

profile of v2, /device:TPU:24, one launch (start us, length us, event | category | flops | bytes accessed | tf_op | source)
XLA Modules:
  0.0 108.8 jit_solution(10029289005517281270)
XLA Ops:
  2.5 3.1 %copy-done = bf16[128,28672]{1,0:T(8,128)(2,1)S(1)} copy-done((bf16[128,28672]{1,0:T(8,128)(2,1)S(1)}, bf16[128,28672]{1,0:T(8,128)(2,1)}, u32[]{:S(2)}) %copy-start) | copy-done | bytes 7340056
  7.4 2.0 %collective-permute-start.6 = (s16[3600,128]{1,0:T(8,128)(2,1)S(1)}, s16[3600,128]{1,0:T(8,128)(2,1)S(1)}, u32[]{:S(2)}, u32[]{:S(2)}) collective-permute-start(s16[3600,128]{1,0:T(8,128)(2,1)S(1)} %get-tuple-element.19.refs_0_.after), channel_id=1, source_target_pairs={{0,32},{16,240},{32,64},{48,16},{64,96},{80,48},{96,128},{112,80},... | collective-permute-start | bytes 2764808 | tf_op jit(solution)/shard_map/ppermute | solution.py:453
  10.1 2.0 %collective-permute-start.8 = (s16[3600,128]{1,0:T(8,128)(2,1)S(1)}, s16[3600,128]{1,0:T(8,128)(2,1)}, u32[]{:S(2)}, u32[]{:S(2)}) collective-permute-start(s16[3600,128]{1,0:T(8,128)(2,1)S(1)} %hop1.1.after.refs_0_), channel_id=1, source_target_pairs={{0,32},{16,240},{32,64},{48,16},{64,96},{80,48},{96,128},{112,80},... | collective-permute-start | bytes 2764808 | tf_op jit(solution)/shard_map/ppermute | solution.py:453
  13.8 3.4 %collective-permute-start.7 = (bf16[128,3584]{1,0:T(8,128)(2,1)}, bf16[128,3584]{1,0:T(8,128)(2,1)}, u32[]{:S(2)}, u32[]{:S(2)}) collective-permute-start(bf16[128,3584]{1,0:T(8,128)(2,1)} %get-tuple-element.25), channel_id=1, source_target_pairs={{0,16},{16,0},{32,48},{48,32},{64,80},{80,64},{96,112},{112,96},{1... | collective-permute-start | bytes 2752520 | tf_op jit(solution)/shard_map/ppermute | solution.py:319
  17.3 7.4 %collective-permute-done.6.refs_4_ = s16[3600,128]{1,0:T(8,128)(2,1)S(1)} collective-permute-done((s16[3600,128]{1,0:T(8,128)(2,1)S(1)}, s16[3600,128]{1,0:T(8,128)(2,1)S(1)}, u32[]{:S(2)}, u32[]{:S(2)}) %collective-permute-start.6) | collective-permute-done | bytes 921632 | tf_op jit(solution)/shard_map/ppermute | solution.py:453
  25.7 2.2 %copy567.1 = (bf16[128,5376]{1,0:T(8,128)(2,1)}, bf16[128,5376]{1,0:T(8,128)(2,1)S(1)}) custom-call(bf16[128,28672]{1,0:T(8,128)(2,1)S(1)} %copy-done.1, s16[3600,128]{1,0:T(8,128)(2,1)S(1)} %hop2.1.refs_0_.after), custom_call_target="tpu_custom_call" | custom-call | flops 235000000 | bytes 1400000 | tf_op jit(solution)/shard_map/copy567/pallas_call | solution.py:331
  28.0 2.2 %collective-permute-start.12 = (bf16[128,5376]{1,0:T(8,128)(2,1)}, bf16[128,5376]{1,0:T(8,128)(2,1)}, u32[]{:S(2)}, u32[]{:S(2)}) collective-permute-start(bf16[128,5376]{1,0:T(8,128)(2,1)} %get-tuple-element.27), channel_id=1, source_target_pairs={{0,16},{16,0},{32,48},{48,32},{64,80},{80,64},{96,112},{112,96},{1... | collective-permute-start | bytes 4128776 | tf_op jit(solution)/shard_map/ppermute | solution.py:319
  32.2 2.5 %collective-permute-done.8.refs_5_ = s16[3600,128]{1,0:T(8,128)(2,1)} collective-permute-done((s16[3600,128]{1,0:T(8,128)(2,1)S(1)}, s16[3600,128]{1,0:T(8,128)(2,1)}, u32[]{:S(2)}, u32[]{:S(2)}) %collective-permute-start.8) | collective-permute-done | bytes 921632 | tf_op jit(solution)/shard_map/ppermute | solution.py:453
  35.9 2.3 %hop3.1.after.refs_0_ = s16[3600,128]{1,0:T(8,128)(2,1)S(1)} custom-call(s16[3600,128]{1,0:T(8,128)(2,1)S(1)} %hop2.1.refs_0_.after, bf16[3584,256]{1,0:T(8,128)(2,1)S(1)} %get-tuple-element.23.refs_1_.basis, bf16[256,256]{1,0:T(8,128)(2,1)S(1)} %get-tuple-element.20.refs_1_.refs_2_.in_t, bf16[128,3584]{1,0:T(8,128)(2,1)S(1)} %copy-done.3, ...), custom_call_target="tpu_custom_call" | custom-call | flops 235000000 | bytes 1400000 | tf_op jit(solution)/shard_map/hop3/pallas_call | solution.py:441
  39.2 5.4 %collective-permute-done.13.refs_5_ = s16[3600,128]{1,0:T(8,128)(2,1)} collective-permute-done((s16[3600,128]{1,0:T(8,128)(2,1)S(1)}, s16[3600,128]{1,0:T(8,128)(2,1)}, u32[]{:S(2)}, u32[]{:S(2)}) %collective-permute-start.13) | collective-permute-done | bytes 921632 | tf_op jit(solution)/shard_map/ppermute | solution.py:453
  44.6 2.2 %hop4.1.refs_0_ = s16[3600,128]{1,0:T(8,128)(2,1)S(1)} custom-call(s16[3600,128]{1,0:T(8,128)(2,1)S(1)} %hop3.1.after.refs_0_, f32[256,1792]{1,0:T(8,128)S(1)} %momentum.1.refs_1_.mom_t, bf16[256,256]{1,0:T(8,128)(2,1)S(1)} %get-tuple-element.20.refs_1_.refs_2_.in_t, bf16[128,3584]{1,0:T(8,128)(2,1)S(1)} %copy-done.3, ...), custom_call_target="tpu_custom_call" | custom-call | flops 235000000 | bytes 1400000 | tf_op jit(solution)/shard_map/hop4/pallas_call | solution.py:441
  48.4 2.7 %collective-permute-start.4 = (f32[28,128]{1,0:T(8,128)S(1)}, f32[28,128]{1,0:T(8,128)S(1)}, u32[]{:S(2)}, u32[]{:S(2)}) collective-permute-start(f32[28,128]{1,0:T(8,128)S(1)} %get-tuple-element.22.k0), channel_id=1, source_target_pairs={{0,2},{1,3},{2,0},{3,1},{4,6},{5,7},{6,4},{7,5},{8,10},{9,11},{10,... | collective-permute-start | bytes 43016 | tf_op jit(solution)/shard_map/ppermute | solution.py:393
  53.6 2.0 %collective-permute-done.5.k3 = f32[28,128]{1,0:T(8,128)S(1)} collective-permute-done((f32[28,128]{1,0:T(8,128)S(1)}, f32[28,128]{1,0:T(8,128)S(1)}, u32[]{:S(2)}, u32[]{:S(2)}) %collective-permute-start.5) | collective-permute-done | bytes 14368 | tf_op jit(solution)/shard_map/ppermute | solution.py:393
  55.7 1.9 %hop5.1.refs_0_ = s16[3600,128]{1,0:T(8,128)(2,1)S(1)} custom-call(s16[3600,128]{1,0:T(8,128)(2,1)S(1)} %hop4.1.refs_0_, f32[4,28,128]{2,1,0:T(8,128)S(1)} %places.1.refs_1_.n0, bf16[256,256]{1,0:T(8,128)(2,1)S(1)} %get-tuple-element.20.refs_1_.refs_2_.in_t, bf16[128,5376]{1,0:T(8,128)(2,1)S(1)} %get-tuple-element.26.refs_3_.own.refs_2_, ...), custom_call_target="tpu_custom_call" | custom-call | flops 235000000 | bytes 1400000 | tf_op jit(solution)/shard_map/hop5/pallas_call | solution.py:441
  57.7 6.5 %collective-permute-done.16.refs_4_ = s16[3600,128]{1,0:T(8,128)(2,1)S(1)} collective-permute-done((s16[3600,128]{1,0:T(8,128)(2,1)S(1)}, s16[3600,128]{1,0:T(8,128)(2,1)S(1)}, u32[]{:S(2)}, u32[]{:S(2)}) %collective-permute-start.16) | collective-permute-done | bytes 921632 | tf_op jit(solution)/shard_map/ppermute | solution.py:453
  64.2 1.9 %hop6.1 = s16[3600,128]{1,0:T(8,128)(2,1)S(1)} custom-call(s16[3600,128]{1,0:T(8,128)(2,1)S(1)} %hop5.1.refs_0_, bf16[256,256]{1,0:T(8,128)(2,1)S(1)} %get-tuple-element.20.refs_1_.refs_2_.in_t, bf16[128,5376]{1,0:T(8,128)(2,1)S(1)} %get-tuple-element.26.refs_3_.own.refs_2_, bf16[128,5376]{1,0:T(8,128)(2,1)} %collective-permute-done.12.refs_4_.sib.refs_3_, ...), custom_call_target="tpu_custom_call" | custom-call | flops 235000000 | bytes 1400000 | tf_op jit(solution)/shard_map/hop6/pallas_call | solution.py:441
  67.5 3.2 %collective-permute-start.9 = (f32[4,28,128]{2,1,0:T(8,128)S(1)}, f32[4,28,128]{2,1,0:T(8,128)S(1)}, u32[]{:S(2)}, u32[]{:S(2)}) collective-permute-start(f32[4,28,128]{2,1,0:T(8,128)S(1)} %places.1.refs_1_.n0), channel_id=1, source_target_pairs={{0,4},{1,5},{2,6},{3,7},{4,8},{5,9},{6,10},{7,11},{8,12},{9,13},{1... | collective-permute-start | bytes 172040 | tf_op jit(solution)/shard_map/ppermute | solution.py:396
  72.0 2.0 %collective-permute-done.11.after3.n3 = f32[4,28,128]{2,1,0:T(8,128)S(1)} collective-permute-done((f32[4,28,128]{2,1,0:T(8,128)S(1)}, f32[4,28,128]{2,1,0:T(8,128)S(1)}, u32[]{:S(2)}, u32[]{:S(2)}) %collective-permute-start.11) | collective-permute-done | bytes 57376 | tf_op jit(solution)/shard_map/ppermute | solution.py:396
  75.7 8.2 %collective-permute-done.17.refs_0_ = s16[3600,128]{1,0:T(8,128)(2,1)S(1)} collective-permute-done((s16[3600,128]{1,0:T(8,128)(2,1)S(1)}, s16[3600,128]{1,0:T(8,128)(2,1)S(1)}, u32[]{:S(2)}, u32[]{:S(2)}) %collective-permute-start.17) | collective-permute-done | bytes 921632 | tf_op jit(solution)/shard_map/ppermute | solution.py:453
  86.7 2.7 %collective-permute-start.19 = (f32[28,128]{1,0:T(8,128)S(1)}, f32[28,128]{1,0:T(8,128)S(1)}, u32[]{:S(2)}, u32[]{:S(2)}) collective-permute-start(f32[28,128]{1,0:T(8,128)S(1)} %get-tuple-element.31.kept.k0), channel_id=1, source_target_pairs={{0,2},{1,3},{2,0},{3,1},{4,6},{5,7},{6,4},{7,5},{8,10},{9,11},{10,... | collective-permute-start | bytes 43016 | tf_op jit(solution)/shard_map/ppermute | solution.py:393
  90.9 3.1 %own.1 = (f32[1792,256]{1,0:T(8,128)}, f32[8,128]{1,0:T(8,128)S(1)}) custom-call(f32[256,1792]{1,0:T(8,128)S(1)} %get-tuple-element.30.updated, f32[28,128]{1,0:T(8,128)S(1)} %get-tuple-element.31.kept.k0, bf16[3584,256]{1,0:T(8,128)(2,1)S(1)} %get-tuple-element.23.refs_1_.basis, f32[896,256]{1,0:T(8,128)S(1)} %get-tuple-element.28.cw), custom_call_target="tpu_custom_call" | custom-call | flops 235000000 | bytes 1400000 | tf_op jit(solution)/shard_map/own/pallas_call | solution.py:482
  94.4 2.6 %collective-permute-start.22 = (f32[4,28,128]{2,1,0:T(8,128)S(1)}, f32[4,28,128]{2,1,0:T(8,128)S(1)}, u32[]{:S(2)}, u32[]{:S(2)}) collective-permute-start(f32[4,28,128]{2,1,0:T(8,128)S(1)} %arrange.1.k0), channel_id=1, source_target_pairs={{0,8},{1,9},{2,10},{3,11},{4,12},{5,13},{6,14},{7,15},{8,0},{9,1},... | collective-permute-start | bytes 172040 | tf_op jit(solution)/shard_map/ppermute | solution.py:396
  100.2 2.3 %collective-permute-done.23.k3 = f32[4,28,128]{2,1,0:T(8,128)S(1)} collective-permute-done((f32[4,28,128]{2,1,0:T(8,128)S(1)}, f32[4,28,128]{2,1,0:T(8,128)S(1)}, u32[]{:S(2)}, u32[]{:S(2)}) %collective-permute-start.23) | collective-permute-done | bytes 57376 | tf_op jit(solution)/shard_map/ppermute | solution.py:396
  102.5 6.4 %update.1 = f32[1792,256]{1,0:T(8,128)} custom-call(f32[4,28,128]{2,1,0:T(8,128)S(1)} %arrange.1.k0, f32[4,28,128]{2,1,0:T(8,128)S(1)} %collective-permute-done.21.k1, f32[4,28,128]{2,1,0:T(8,128)S(1)} %collective-permute-done.22.k2, f32[4,28,128]{2,1,0:T(8,128)S(1)} %collective-permute-done.23.k3, f32[4,28,128]{2,1,0:T(8,128)S(1)} %places.1.refs_1_.n0, ...), custom_call_target="tpu_custom_call" | custom-call | flops 235000000 | bytes 1400000 | tf_op jit(solution)/shard_map/update/pallas_call | solution.py:498
  (66 shorter events, 27.7 us)
Async XLA Ops:
  1.9 4.7 %collective-permute-start.1 = (bf16[128,1792]{1,0:T(8,128)(2,1)S(1)}, bf16[128,1792]{1,0:T(8,128)(2,1)S(1)}, u32[]{:S(2)}, u32[]{:S(2)}) collective-permute-start(bf16[128,1792]{1,0:T(8,128)(2,1)S(1)} %get-tuple-element.34.after), channel_id=1, source_target_pairs={{0,16},{16,0},{32,48},{48,32},{64,80},{80,64},{96,112},{112,96},{1... | collective-permute-start | bytes 1376264 | tf_op jit(solution)/shard_map/ppermute | solution.py:319
  2.0 4.6 %collective-permute-start = (bf16[128,256]{1,0:T(8,128)(2,1)S(1)}, bf16[128,256]{1,0:T(8,128)(2,1)S(1)}, u32[]{:S(2)}, u32[]{:S(2)}) collective-permute-start(bf16[128,256]{1,0:T(8,128)(2,1)S(1)} %copy-done.6), channel_id=1, source_target_pairs={{0,16},{16,0},{32,48},{48,32},{64,80},{80,64},{96,112},{112,96},{1... | collective-permute-start | bytes 196616 | tf_op jit(solution)/shard_map/ppermute | solution.py:319
  6.4 3.0 %collective-permute-start.2 = (bf16[128,3584]{1,0:T(8,128)(2,1)S(1)}, bf16[128,3584]{1,0:T(8,128)(2,1)S(1)}, u32[]{:S(2)}, u32[]{:S(2)}) collective-permute-start(bf16[128,3584]{1,0:T(8,128)(2,1)S(1)} %get-tuple-element.18.after), channel_id=1, source_target_pairs={{0,16},{16,0},{32,48},{48,32},{64,80},{80,64},{96,112},{112,96},{1... | collective-permute-start | bytes 2752520 | tf_op jit(solution)/shard_map/ppermute | solution.py:319
  7.4 17.3 %collective-permute-start.6 = (s16[3600,128]{1,0:T(8,128)(2,1)S(1)}, s16[3600,128]{1,0:T(8,128)(2,1)S(1)}, u32[]{:S(2)}, u32[]{:S(2)}) collective-permute-start(s16[3600,128]{1,0:T(8,128)(2,1)S(1)} %get-tuple-element.19.refs_0_.after), channel_id=1, source_target_pairs={{0,32},{16,240},{32,64},{48,16},{64,96},{80,48},{96,128},{112,80},... | collective-permute-start | bytes 2764808 | tf_op jit(solution)/shard_map/ppermute | solution.py:453
  10.1 24.6 %collective-permute-start.8 = (s16[3600,128]{1,0:T(8,128)(2,1)S(1)}, s16[3600,128]{1,0:T(8,128)(2,1)}, u32[]{:S(2)}, u32[]{:S(2)}) collective-permute-start(s16[3600,128]{1,0:T(8,128)(2,1)S(1)} %hop1.1.after.refs_0_), channel_id=1, source_target_pairs={{0,32},{16,240},{32,64},{48,16},{64,96},{80,48},{96,128},{112,80},... | collective-permute-start | bytes 2764808 | tf_op jit(solution)/shard_map/ppermute | solution.py:453
  13.8 18.3 %collective-permute-start.7 = (bf16[128,3584]{1,0:T(8,128)(2,1)}, bf16[128,3584]{1,0:T(8,128)(2,1)}, u32[]{:S(2)}, u32[]{:S(2)}) collective-permute-start(bf16[128,3584]{1,0:T(8,128)(2,1)} %get-tuple-element.25), channel_id=1, source_target_pairs={{0,16},{16,0},{32,48},{48,32},{64,80},{80,64},{96,112},{112,96},{1... | collective-permute-start | bytes 2752520 | tf_op jit(solution)/shard_map/ppermute | solution.py:319
  25.6 18.9 %collective-permute-start.13 = (s16[3600,128]{1,0:T(8,128)(2,1)S(1)}, s16[3600,128]{1,0:T(8,128)(2,1)}, u32[]{:S(2)}, u32[]{:S(2)}) collective-permute-start(s16[3600,128]{1,0:T(8,128)(2,1)S(1)} %hop2.1.refs_0_.after), channel_id=1, source_target_pairs={{0,32},{16,240},{32,64},{48,16},{64,96},{80,48},{96,128},{112,80},... | collective-permute-start | bytes 2764808 | tf_op jit(solution)/shard_map/ppermute | solution.py:453
  28.0 27.7 %collective-permute-start.12 = (bf16[128,5376]{1,0:T(8,128)(2,1)}, bf16[128,5376]{1,0:T(8,128)(2,1)}, u32[]{:S(2)}, u32[]{:S(2)}) collective-permute-start(bf16[128,5376]{1,0:T(8,128)(2,1)} %get-tuple-element.27), channel_id=1, source_target_pairs={{0,16},{16,0},{32,48},{48,32},{64,80},{80,64},{96,112},{112,96},{1... | collective-permute-start | bytes 4128776 | tf_op jit(solution)/shard_map/ppermute | solution.py:319
  38.2 17.6 %collective-permute-start.14 = (s16[3600,128]{1,0:T(8,128)(2,1)S(1)}, s16[3600,128]{1,0:T(8,128)(2,1)S(1)}, u32[]{:S(2)}, u32[]{:S(2)}) collective-permute-start(s16[3600,128]{1,0:T(8,128)(2,1)S(1)} %hop3.1.after.refs_0_), channel_id=1, source_target_pairs={{0,32},{16,240},{32,64},{48,16},{64,96},{80,48},{96,128},{112,80},... | collective-permute-start | bytes 2764808 | tf_op jit(solution)/shard_map/ppermute | solution.py:453
  46.7 17.5 %collective-permute-start.16 = (s16[3600,128]{1,0:T(8,128)(2,1)S(1)}, s16[3600,128]{1,0:T(8,128)(2,1)S(1)}, u32[]{:S(2)}, u32[]{:S(2)}) collective-permute-start(s16[3600,128]{1,0:T(8,128)(2,1)S(1)} %hop4.1.refs_0_), channel_id=1, source_target_pairs={{0,32},{16,240},{32,64},{48,16},{64,96},{80,48},{96,128},{112,80},... | collective-permute-start | bytes 2764808 | tf_op jit(solution)/shard_map/ppermute | solution.py:453
  46.8 5.0 %collective-permute-start.3 = (f32[28,128]{1,0:T(8,128)S(1)}, f32[28,128]{1,0:T(8,128)S(1)}, u32[]{:S(2)}, u32[]{:S(2)}) collective-permute-start(f32[28,128]{1,0:T(8,128)S(1)} %get-tuple-element.22.k0), channel_id=1, source_target_pairs={{0,1},{1,2},{2,3},{3,0},{4,5},{5,6},{6,7},{7,4},{8,9},{9,10},{10,1... | collective-permute-start | bytes 43016 | tf_op jit(solution)/shard_map/ppermute | solution.py:393
  48.4 5.2 %collective-permute-start.4 = (f32[28,128]{1,0:T(8,128)S(1)}, f32[28,128]{1,0:T(8,128)S(1)}, u32[]{:S(2)}, u32[]{:S(2)}) collective-permute-start(f32[28,128]{1,0:T(8,128)S(1)} %get-tuple-element.22.k0), channel_id=1, source_target_pairs={{0,2},{1,3},{2,0},{3,1},{4,6},{5,7},{6,4},{7,5},{8,10},{9,11},{10,... | collective-permute-start | bytes 43016 | tf_op jit(solution)/shard_map/ppermute | solution.py:393
  51.9 3.7 %collective-permute-start.5 = (f32[28,128]{1,0:T(8,128)S(1)}, f32[28,128]{1,0:T(8,128)S(1)}, u32[]{:S(2)}, u32[]{:S(2)}) collective-permute-start(f32[28,128]{1,0:T(8,128)S(1)} %get-tuple-element.22.k0), channel_id=1, source_target_pairs={{0,3},{1,0},{2,1},{3,2},{4,7},{5,4},{6,5},{7,6},{8,11},{9,8},{10,9... | collective-permute-start | bytes 43016 | tf_op jit(solution)/shard_map/ppermute | solution.py:393
  57.6 16.4 %collective-permute-start.15 = (s16[3600,128]{1,0:T(8,128)(2,1)S(1)}, s16[3600,128]{1,0:T(8,128)(2,1)S(1)}, u32[]{:S(2)}, u32[]{:S(2)}) collective-permute-start(s16[3600,128]{1,0:T(8,128)(2,1)S(1)} %hop5.1.refs_0_), channel_id=1, source_target_pairs={{0,48},{16,224},{32,80},{48,0},{64,112},{80,32},{96,144},{112,64},... | collective-permute-start | bytes 2764808 | tf_op jit(solution)/shard_map/ppermute | solution.py:453
  66.1 17.9 %collective-permute-start.17 = (s16[3600,128]{1,0:T(8,128)(2,1)S(1)}, s16[3600,128]{1,0:T(8,128)(2,1)S(1)}, u32[]{:S(2)}, u32[]{:S(2)}) collective-permute-start(s16[3600,128]{1,0:T(8,128)(2,1)S(1)} %hop6.1), channel_id=1, source_target_pairs={{0,32},{16,240},{32,64},{48,16},{64,96},{80,48},{96,128},{112,80},... | collective-permute-start | bytes 2764808 | tf_op jit(solution)/shard_map/ppermute | solution.py:453
  66.2 5.9 %collective-permute-start.10 = (f32[4,28,128]{2,1,0:T(8,128)S(1)}, f32[4,28,128]{2,1,0:T(8,128)S(1)}, u32[]{:S(2)}, u32[]{:S(2)}) collective-permute-start(f32[4,28,128]{2,1,0:T(8,128)S(1)} %places.1.refs_1_.n0), channel_id=1, source_target_pairs={{0,8},{1,9},{2,10},{3,11},{4,12},{5,13},{6,14},{7,15},{8,0},{9,1},... | collective-permute-start | bytes 172040 | tf_op jit(solution)/shard_map/ppermute | solution.py:396
  67.5 6.5 %collective-permute-start.11 = (f32[4,28,128]{2,1,0:T(8,128)S(1)}, f32[4,28,128]{2,1,0:T(8,128)S(1)}, u32[]{:S(2)}, u32[]{:S(2)}) collective-permute-start(f32[4,28,128]{2,1,0:T(8,128)S(1)} %places.1.refs_1_.n0), channel_id=1, source_target_pairs={{0,12},{1,13},{2,14},{3,15},{4,0},{5,1},{6,2},{7,3},{8,4},{9,5},{1... | collective-permute-start | bytes 172040 | tf_op jit(solution)/shard_map/ppermute | solution.py:396
  67.5 6.5 %collective-permute-start.9 = (f32[4,28,128]{2,1,0:T(8,128)S(1)}, f32[4,28,128]{2,1,0:T(8,128)S(1)}, u32[]{:S(2)}, u32[]{:S(2)}) collective-permute-start(f32[4,28,128]{2,1,0:T(8,128)S(1)} %places.1.refs_1_.n0), channel_id=1, source_target_pairs={{0,4},{1,5},{2,6},{3,7},{4,8},{5,9},{6,10},{7,11},{8,12},{9,13},{1... | collective-permute-start | bytes 172040 | tf_op jit(solution)/shard_map/ppermute | solution.py:396
  85.2 8.8 %collective-permute-start.18 = (f32[28,128]{1,0:T(8,128)S(1)}, f32[28,128]{1,0:T(8,128)S(1)}, u32[]{:S(2)}, u32[]{:S(2)}) collective-permute-start(f32[28,128]{1,0:T(8,128)S(1)} %get-tuple-element.31.kept.k0), channel_id=1, source_target_pairs={{0,1},{1,2},{2,3},{3,0},{4,5},{5,6},{6,7},{7,4},{8,9},{9,10},{10,1... | collective-permute-start | bytes 43016 | tf_op jit(solution)/shard_map/ppermute | solution.py:393
  86.7 7.3 %collective-permute-start.19 = (f32[28,128]{1,0:T(8,128)S(1)}, f32[28,128]{1,0:T(8,128)S(1)}, u32[]{:S(2)}, u32[]{:S(2)}) collective-permute-start(f32[28,128]{1,0:T(8,128)S(1)} %get-tuple-element.31.kept.k0), channel_id=1, source_target_pairs={{0,2},{1,3},{2,0},{3,1},{4,6},{5,7},{6,4},{7,5},{8,10},{9,11},{10,... | collective-permute-start | bytes 43016 | tf_op jit(solution)/shard_map/ppermute | solution.py:393
  89.4 4.5 %collective-permute-start.20 = (f32[28,128]{1,0:T(8,128)S(1)}, f32[28,128]{1,0:T(8,128)S(1)}, u32[]{:S(2)}, u32[]{:S(2)}) collective-permute-start(f32[28,128]{1,0:T(8,128)S(1)} %get-tuple-element.31.kept.k0), channel_id=1, source_target_pairs={{0,3},{1,0},{2,1},{3,2},{4,7},{5,4},{6,5},{7,6},{8,11},{9,8},{10,9... | collective-permute-start | bytes 43016 | tf_op jit(solution)/shard_map/ppermute | solution.py:393
  94.1 4.3 %collective-permute-start.21 = (f32[4,28,128]{2,1,0:T(8,128)S(1)}, f32[4,28,128]{2,1,0:T(8,128)S(1)}, u32[]{:S(2)}, u32[]{:S(2)}) collective-permute-start(f32[4,28,128]{2,1,0:T(8,128)S(1)} %arrange.1.k0), channel_id=1, source_target_pairs={{0,4},{1,5},{2,6},{3,7},{4,8},{5,9},{6,10},{7,11},{8,12},{9,13},{1... | collective-permute-start | bytes 172040 | tf_op jit(solution)/shard_map/ppermute | solution.py:396
  94.4 5.8 %collective-permute-start.22 = (f32[4,28,128]{2,1,0:T(8,128)S(1)}, f32[4,28,128]{2,1,0:T(8,128)S(1)}, u32[]{:S(2)}, u32[]{:S(2)}) collective-permute-start(f32[4,28,128]{2,1,0:T(8,128)S(1)} %arrange.1.k0), channel_id=1, source_target_pairs={{0,8},{1,9},{2,10},{3,11},{4,12},{5,13},{6,14},{7,15},{8,0},{9,1},... | collective-permute-start | bytes 172040 | tf_op jit(solution)/shard_map/ppermute | solution.py:396
  97.0 5.5 %collective-permute-start.23 = (f32[4,28,128]{2,1,0:T(8,128)S(1)}, f32[4,28,128]{2,1,0:T(8,128)S(1)}, u32[]{:S(2)}, u32[]{:S(2)}) collective-permute-start(f32[4,28,128]{2,1,0:T(8,128)S(1)} %arrange.1.k0), channel_id=1, source_target_pairs={{0,12},{1,13},{2,14},{3,15},{4,0},{5,1},{6,2},{7,3},{8,4},{9,5},{1... | collective-permute-start | bytes 172040 | tf_op jit(solution)/shard_map/ppermute | solution.py:396
  (11 other events, 63.7 us)

commit v3 on v2

--- a/solution.py
+++ b/solution.py
@@ -142,7 +142,7 @@
         c.wait()
 
 
-def first_hop_kernel(in_own, in_sib, own, sib, after, in_t, *outs):
+def first_hop_kernel(in_own, in_sib, own, sib, in_t, *outs):
     in_t[:, :TOK] = in_own[...].astype(F32).T.astype(BF16)
     in_t[:, TOK:] = in_sib[...].astype(F32).T.astype(BF16)
     both = in_t[...]
@@ -341,14 +341,17 @@
         return send
 
     place = lax.axis_index("fsdp")
-    across = (place + CHIPS) % (2 * CHIPS)
-    first, first_own = (
-        lax.dynamic_slice(cotangent, (0, block * ROWS), (TOK, ROWS))
-        for block in (across ^ 1, across)
-    )
-    exchanged(first, first_own, 1)
+
+    def sliced(slot, whose):
+        k, flip = SLOTS[slot]
+        to = (place // 2 + k * (1 - 2 * whose) + CHIPS) % CHIPS
+        start = (2 * to + (1 - whose if flip else whose)) * ROWS
+        return lax.dynamic_slice(cotangent, (0, start), (TOK, ROWS))
+
+    exchanged(sliced(0, 1 - place % 2), sliced(0, place % 2), 1)
     in_sib = swap(inputs)
-    second = copied(1, 3, first, "copy12")
+    for slot in (1, 2):
+        exchanged(sliced(slot, 1 - place % 2), sliced(slot, place % 2), 1)
 
     def blocks(slot):
         specs, args = [], []
@@ -420,10 +423,9 @@
                 "hop0",
                 (1,),
                 [whole(TOK, COLS), whole(TOK, COLS)]
-                + specs
-                + [AFTER],
+                + specs,
                 (whole(COLS, 2 * TOK),) + out_specs,
-            )(inputs, in_sib, *args, second)
+            )(inputs, in_sib, *args)
         else:
             recv, recv_specs = ((), ()) if slot < 2 else (sent[slot - 2], message(slot - 2)[1])
             after = (made[-1],)

time: 109 us -> 107 us (0.982)
  waiting for transfers between devices: 41.7 us -> 45.5 us
  starting transfers between devices: 30 us -> 27.5 us
  local copies, waits for them, and re-layouts: 5.65 us -> 3.38 us
    unnamed x22 -> x20, local copies, waits for them, and re-layouts: 4.33 us -> 1.22 us
    ppermute x5 -> x6, waiting for transfers between devices: 0.01 us -> 2.85 us  [on_device(): lax.ppermute(x, 'fsdp', [(i, i ^ 1) for i in range(2 * CHIPS)])]
    ppermute x6, waiting for transfers between devices: 8.74 us -> 11.3 us  [along_y(): lax.ppermute(rows, 'rep', rep_perm(0, dy))]
    ppermute x7, starting transfers between devices: 4.59 us -> 2.68 us  [on_device(): lax.ppermute(out, 'fsdp', ring_perm(slot == 5))]
    ppermute x7, waiting for transfers between devices: 30 us -> 28.2 us  [on_device(): lax.ppermute(out, 'fsdp', ring_perm(slot == 5))]
    ppermute x6, starting transfers between devices: 7.45 us -> 5.78 us  [along_y(): lax.ppermute(rows, 'rep', rep_perm(0, dy))]
    ppermute x5 -> x6, starting transfers between devices: 6.44 us -> 7.48 us  [on_device(): lax.ppermute(x, 'fsdp', [(i, i ^ 1) for i in range(2 * CHIPS)])]
    pallas_call x3 -> x2, Pallas kernels: 4.67 us -> 3.96 us  [copied(): call(functools.partial(copy_kernel, SLOTS[begin:end]), (shape, shape), na...]
  transfers between devices with their start and end apart: 24 -> 25, of which waited for: 13 -> 16; matrix products, arithmetic and copies ran while one was open for 0% -> 0% of each run, Pallas kernels for 21% -> 20%
where the time goes in v3:
time: 107 us
  waiting for transfers between devices  45.5 us (43%)
  Pallas kernels  29.7 us (28%)
  starting transfers between devices  27.5 us (26%)
  local copies, waits for them, and re-layouts  3.38 us (3%)
    ppermute x7, waiting for transfers between devices, on_device(): lax.ppermute(out, 'fsdp', ring_perm(slot == 5))  28.2 us
    ppermute x6, starting transfers between devices, along_x(): return [lax.ppermute(rows, 'rep', rep_perm(dx, 0)) for dx in (1, 2, 3)]  11.6 us
    ppermute x6, waiting for transfers between devices, along_y(): lax.ppermute(rows, 'rep', rep_perm(0, dy))  11.3 us
    pallas_call x6, Pallas kernels, on_device(): call(functools.partial(hop_kernel, len(after), len(recv)), shapes, 'hop%d...  9.78 us
    ppermute x6, starting transfers between devices, on_device(): lax.ppermute(x, 'fsdp', [(i, i ^ 1) for i in range(2 * CHIPS)])  7.48 us
    pallas_call x1, Pallas kernels, on_device(): call(update_kernel, jax.ShapeDtypeStruct((ROWS, COLS), F32), 'update', (2...  6.38 us
    ppermute x6, starting transfers between devices, along_y(): lax.ppermute(rows, 'rep', rep_perm(0, dy))  5.78 us
    pallas_call x2, Pallas kernels, copied(): call(functools.partial(copy_kernel, SLOTS[begin:end]), (shape, shape), na...  3.96 us
  transfers between devices with their start and end apart: 25, of which 16 were waited for; matrix products, arithmetic and copies ran while one was open for 0% of the time, Pallas kernels for 20%

profile of v3, /device:TPU:24, one launch (start us, length us, event | category | flops | bytes accessed | tf_op | source)
XLA Modules:
  0.0 107.2 jit_solution(16912033170286033808)
XLA Ops:
  0.8 2.1 %constant_dynamic-slice_fusion = (bf16[128,1792]{1,0:T(8,128)(2,1)S(1)}, bf16[128,1792]{1,0:T(8,128)(2,1)S(1)}, bf16[128,1792]{1,0:T(8,128)(2,1)S(1)}, bf16[128,...) fusion(bf16[128,28672]{1,0:T(8,128)(2,1)} %cot.3, s32[]{:T(128)S(6)} %select_n.75, ...), kind=kLoop, calls=%fused_computation | loop fusion | bytes 5505048 | tf_op jit(solution)/shard_map/dynamic_slice | solution.py:349
  5.6 2.0 %collective-permute-start.7 = (s16[3600,128]{1,0:T(8,128)(2,1)S(1)}, s16[3600,128]{1,0:T(8,128)(2,1)S(1)}, u32[]{:S(2)}, u32[]{:S(2)}) collective-permute-start(s16[3600,128]{1,0:T(8,128)(2,1)S(1)} %get-tuple-element.16.refs_0_.after), channel_id=1, source_target_pairs={{0,32},{16,240},{32,64},{48,16},{64,96},{80,48},{96,128},{112,80},... | collective-permute-start | bytes 2764808 | tf_op jit(solution)/shard_map/ppermute | solution.py:455
  7.6 3.8 %collective-permute-start.2 = (bf16[128,1792]{1,0:T(8,128)(2,1)S(1)}, bf16[128,1792]{1,0:T(8,128)(2,1)S(1)}, u32[]{:S(2)}, u32[]{:S(2)}) collective-permute-start(bf16[128,1792]{1,0:T(8,128)(2,1)S(1)} %get-tuple-element.32), channel_id=1, source_target_pairs={{0,16},{16,0},{32,48},{48,32},{64,80},{80,64},{96,112},{112,96},{1... | collective-permute-start | bytes 1376264 | tf_op jit(solution)/shard_map/ppermute | solution.py:319
  16.6 6.4 %collective-permute-done.7.refs_4_ = s16[3600,128]{1,0:T(8,128)(2,1)S(1)} collective-permute-done((s16[3600,128]{1,0:T(8,128)(2,1)S(1)}, s16[3600,128]{1,0:T(8,128)(2,1)S(1)}, u32[]{:S(2)}, u32[]{:S(2)}) %collective-permute-start.7) | collective-permute-done | bytes 921632 | tf_op jit(solution)/shard_map/ppermute | solution.py:455
  24.0 2.2 %copy567.1 = (bf16[128,5376]{1,0:T(8,128)(2,1)}, bf16[128,5376]{1,0:T(8,128)(2,1)S(1)}) custom-call(bf16[128,28672]{1,0:T(8,128)(2,1)S(1)} %copy-done, s16[3600,128]{1,0:T(8,128)(2,1)S(1)} %hop2.1.refs_0_.after), custom_call_target="tpu_custom_call" | custom-call | flops 235000000 | bytes 1400000 | tf_op jit(solution)/shard_map/copy567/pallas_call | solution.py:331
  26.2 2.0 %collective-permute-start.13 = (bf16[128,5376]{1,0:T(8,128)(2,1)}, bf16[128,5376]{1,0:T(8,128)(2,1)}, u32[]{:S(2)}, u32[]{:S(2)}) collective-permute-start(bf16[128,5376]{1,0:T(8,128)(2,1)} %get-tuple-element.23), channel_id=1, source_target_pairs={{0,16},{16,0},{32,48},{48,32},{64,80},{80,64},{96,112},{112,96},{1... | collective-permute-start | bytes 4128776 | tf_op jit(solution)/shard_map/ppermute | solution.py:319
  28.3 1.9 %tables.1 = (bf16[3584,256]{1,0:T(8,128)(2,1)S(1)}, f32[896,256]{1,0:T(8,128)S(1)}, f32[28,128]{1,0:T(8,128)S(1)}, f32[28,128]{1,0:T(8,128)S(1)}) custom-call(s32[28,4,32]{2,1,0:T(4,128)S(1)} %bitcast.5, s32[28,4]{1,0:T(8,128)S(1)} %copy.10.counts, f32[64,64]{1,0:T(8,128)S(1)} %copy-done.8, s16[3600,128]{1,0:T(8,128)(2,1)S(1)} %hop1.1.after.refs_0_), custom_call_target="tpu_custom_call" | custom-call | flops 235000000 | bytes 1400000 | tf_op jit(solution)/shard_map/tables/pallas_call | solution.py:371
  30.2 2.8 %collective-permute-done.9.refs_5_ = s16[3600,128]{1,0:T(8,128)(2,1)} collective-permute-done((s16[3600,128]{1,0:T(8,128)(2,1)S(1)}, s16[3600,128]{1,0:T(8,128)(2,1)}, u32[]{:S(2)}, u32[]{:S(2)}) %collective-permute-start.9) | collective-permute-done | bytes 921632 | tf_op jit(solution)/shard_map/ppermute | solution.py:455
  34.2 2.3 %hop3.1.after.refs_0_ = s16[3600,128]{1,0:T(8,128)(2,1)S(1)} custom-call(s16[3600,128]{1,0:T(8,128)(2,1)S(1)} %hop2.1.refs_0_.after, bf16[3584,256]{1,0:T(8,128)(2,1)S(1)} %get-tuple-element.19.refs_1_.basis, bf16[256,256]{1,0:T(8,128)(2,1)S(1)} %get-tuple-element.17.refs_1_.refs_2_.in_t, bf16[128,3584]{1,0:T(8,128)(2,1)S(1)} %copy-done.2, ...), custom_call_target="tpu_custom_call" | custom-call | flops 235000000 | bytes 1400000 | tf_op jit(solution)/shard_map/hop3/pallas_call | solution.py:443
  37.5 5.4 %collective-permute-done.14.refs_5_ = s16[3600,128]{1,0:T(8,128)(2,1)} collective-permute-done((s16[3600,128]{1,0:T(8,128)(2,1)S(1)}, s16[3600,128]{1,0:T(8,128)(2,1)}, u32[]{:S(2)}, u32[]{:S(2)}) %collective-permute-start.14) | collective-permute-done | bytes 921632 | tf_op jit(solution)/shard_map/ppermute | solution.py:455
  42.8 2.2 %hop4.1.refs_0_ = s16[3600,128]{1,0:T(8,128)(2,1)S(1)} custom-call(s16[3600,128]{1,0:T(8,128)(2,1)S(1)} %hop3.1.after.refs_0_, f32[256,1792]{1,0:T(8,128)S(1)} %momentum.1.refs_1_.mom_t, bf16[256,256]{1,0:T(8,128)(2,1)S(1)} %get-tuple-element.17.refs_1_.refs_2_.in_t, bf16[128,3584]{1,0:T(8,128)(2,1)S(1)} %copy-done.2, ...), custom_call_target="tpu_custom_call" | custom-call | flops 235000000 | bytes 1400000 | tf_op jit(solution)/shard_map/hop4/pallas_call | solution.py:443
  46.7 2.7 %collective-permute-start.4 = (f32[28,128]{1,0:T(8,128)S(1)}, f32[28,128]{1,0:T(8,128)S(1)}, u32[]{:S(2)}, u32[]{:S(2)}) collective-permute-start(f32[28,128]{1,0:T(8,128)S(1)} %get-tuple-element.18.k0), channel_id=1, source_target_pairs={{0,2},{1,3},{2,0},{3,1},{4,6},{5,7},{6,4},{7,5},{8,10},{9,11},{10,... | collective-permute-start | bytes 43016 | tf_op jit(solution)/shard_map/ppermute | solution.py:396
  52.0 2.0 %collective-permute-done.5.k3 = f32[28,128]{1,0:T(8,128)S(1)} collective-permute-done((f32[28,128]{1,0:T(8,128)S(1)}, f32[28,128]{1,0:T(8,128)S(1)}, u32[]{:S(2)}, u32[]{:S(2)}) %collective-permute-start.5) | collective-permute-done | bytes 14368 | tf_op jit(solution)/shard_map/ppermute | solution.py:396
  54.2 1.9 %hop5.1.refs_0_ = s16[3600,128]{1,0:T(8,128)(2,1)S(1)} custom-call(s16[3600,128]{1,0:T(8,128)(2,1)S(1)} %hop4.1.refs_0_, f32[4,28,128]{2,1,0:T(8,128)S(1)} %places.1.refs_1_.n0, bf16[256,256]{1,0:T(8,128)(2,1)S(1)} %get-tuple-element.17.refs_1_.refs_2_.in_t, bf16[128,5376]{1,0:T(8,128)(2,1)S(1)} %get-tuple-element.22.refs_3_.own.refs_2_, ...), custom_call_target="tpu_custom_call" | custom-call | flops 235000000 | bytes 1400000 | tf_op jit(solution)/shard_map/hop5/pallas_call | solution.py:443
  56.2 6.3 %collective-permute-done.17.refs_4_ = s16[3600,128]{1,0:T(8,128)(2,1)S(1)} collective-permute-done((s16[3600,128]{1,0:T(8,128)(2,1)S(1)}, s16[3600,128]{1,0:T(8,128)(2,1)S(1)}, u32[]{:S(2)}, u32[]{:S(2)}) %collective-permute-start.17) | collective-permute-done | bytes 921632 | tf_op jit(solution)/shard_map/ppermute | solution.py:455
  62.5 1.9 %hop6.1 = s16[3600,128]{1,0:T(8,128)(2,1)S(1)} custom-call(s16[3600,128]{1,0:T(8,128)(2,1)S(1)} %hop5.1.refs_0_, bf16[256,256]{1,0:T(8,128)(2,1)S(1)} %get-tuple-element.17.refs_1_.refs_2_.in_t, bf16[128,5376]{1,0:T(8,128)(2,1)S(1)} %get-tuple-element.22.refs_3_.own.refs_2_, bf16[128,5376]{1,0:T(8,128)(2,1)} %collective-permute-done.13.refs_4_.sib.refs_3_, ...), custom_call_target="tpu_custom_call" | custom-call | flops 235000000 | bytes 1400000 | tf_op jit(solution)/shard_map/hop6/pallas_call | solution.py:443
  64.8 2.6 %collective-permute-start.11 = (f32[4,28,128]{2,1,0:T(8,128)S(1)}, f32[4,28,128]{2,1,0:T(8,128)S(1)}, u32[]{:S(2)}, u32[]{:S(2)}) collective-permute-start(f32[4,28,128]{2,1,0:T(8,128)S(1)} %places.1.refs_1_.n0), channel_id=1, source_target_pairs={{0,8},{1,9},{2,10},{3,11},{4,12},{5,13},{6,14},{7,15},{8,0},{9,1},... | collective-permute-start | bytes 172040 | tf_op jit(solution)/shard_map/ppermute | solution.py:399
  70.6 2.6 %collective-permute-done.12.after3.n3 = f32[4,28,128]{2,1,0:T(8,128)S(1)} collective-permute-done((f32[4,28,128]{2,1,0:T(8,128)S(1)}, f32[4,28,128]{2,1,0:T(8,128)S(1)}, u32[]{:S(2)}, u32[]{:S(2)}) %collective-permute-start.12) | collective-permute-done | bytes 57376 | tf_op jit(solution)/shard_map/ppermute | solution.py:399
  74.9 7.3 %collective-permute-done.18.refs_0_ = s16[3600,128]{1,0:T(8,128)(2,1)S(1)} collective-permute-done((s16[3600,128]{1,0:T(8,128)(2,1)S(1)}, s16[3600,128]{1,0:T(8,128)(2,1)S(1)}, u32[]{:S(2)}, u32[]{:S(2)}) %collective-permute-start.18) | collective-permute-done | bytes 921632 | tf_op jit(solution)/shard_map/ppermute | solution.py:455
  85.0 2.7 %collective-permute-start.20 = (f32[28,128]{1,0:T(8,128)S(1)}, f32[28,128]{1,0:T(8,128)S(1)}, u32[]{:S(2)}, u32[]{:S(2)}) collective-permute-start(f32[28,128]{1,0:T(8,128)S(1)} %get-tuple-element.27.kept.k0), channel_id=1, source_target_pairs={{0,2},{1,3},{2,0},{3,1},{4,6},{5,7},{6,4},{7,5},{8,10},{9,11},{10,... | collective-permute-start | bytes 43016 | tf_op jit(solution)/shard_map/ppermute | solution.py:396
  89.2 3.1 %own.1 = (f32[1792,256]{1,0:T(8,128)}, f32[8,128]{1,0:T(8,128)S(1)}) custom-call(f32[256,1792]{1,0:T(8,128)S(1)} %get-tuple-element.26.updated, f32[28,128]{1,0:T(8,128)S(1)} %get-tuple-element.27.kept.k0, bf16[3584,256]{1,0:T(8,128)(2,1)S(1)} %get-tuple-element.19.refs_1_.basis, f32[896,256]{1,0:T(8,128)S(1)} %get-tuple-element.24.cw), custom_call_target="tpu_custom_call" | custom-call | flops 235000000 | bytes 1400000 | tf_op jit(solution)/shard_map/own/pallas_call | solution.py:484
  92.7 2.6 %collective-permute-start.23 = (f32[4,28,128]{2,1,0:T(8,128)S(1)}, f32[4,28,128]{2,1,0:T(8,128)S(1)}, u32[]{:S(2)}, u32[]{:S(2)}) collective-permute-start(f32[4,28,128]{2,1,0:T(8,128)S(1)} %arrange.1.k0), channel_id=1, source_target_pairs={{0,8},{1,9},{2,10},{3,11},{4,12},{5,13},{6,14},{7,15},{8,0},{9,1},... | collective-permute-start | bytes 172040 | tf_op jit(solution)/shard_map/ppermute | solution.py:399
  98.5 2.3 %collective-permute-done.24.k3 = f32[4,28,128]{2,1,0:T(8,128)S(1)} collective-permute-done((f32[4,28,128]{2,1,0:T(8,128)S(1)}, f32[4,28,128]{2,1,0:T(8,128)S(1)}, u32[]{:S(2)}, u32[]{:S(2)}) %collective-permute-start.24) | collective-permute-done | bytes 57376 | tf_op jit(solution)/shard_map/ppermute | solution.py:399
  100.8 6.4 %update.1 = f32[1792,256]{1,0:T(8,128)} custom-call(f32[4,28,128]{2,1,0:T(8,128)S(1)} %arrange.1.k0, f32[4,28,128]{2,1,0:T(8,128)S(1)} %collective-permute-done.22.k1, f32[4,28,128]{2,1,0:T(8,128)S(1)} %collective-permute-done.23.k2, f32[4,28,128]{2,1,0:T(8,128)S(1)} %collective-permute-done.24.k3, f32[4,28,128]{2,1,0:T(8,128)S(1)} %places.1.refs_1_.n0, ...), custom_call_target="tpu_custom_call" | custom-call | flops 235000000 | bytes 1400000 | tf_op jit(solution)/shard_map/update/pallas_call | solution.py:500
  (65 shorter events, 28.7 us)
Async XLA Ops:
  2.8 2.0 %collective-permute-start.1 = (bf16[128,1792]{1,0:T(8,128)(2,1)S(1)}, bf16[128,1792]{1,0:T(8,128)(2,1)S(1)}, u32[]{:S(2)}, u32[]{:S(2)}) collective-permute-start(bf16[128,1792]{1,0:T(8,128)(2,1)S(1)} %get-tuple-element.34), channel_id=1, source_target_pairs={{0,16},{16,0},{32,48},{48,32},{64,80},{80,64},{96,112},{112,96},{1... | collective-permute-start | bytes 1376264 | tf_op jit(solution)/shard_map/ppermute | solution.py:319
  5.6 17.3 %collective-permute-start.7 = (s16[3600,128]{1,0:T(8,128)(2,1)S(1)}, s16[3600,128]{1,0:T(8,128)(2,1)S(1)}, u32[]{:S(2)}, u32[]{:S(2)}) collective-permute-start(s16[3600,128]{1,0:T(8,128)(2,1)S(1)} %get-tuple-element.16.refs_0_.after), channel_id=1, source_target_pairs={{0,32},{16,240},{32,64},{48,16},{64,96},{80,48},{96,128},{112,80},... | collective-permute-start | bytes 2764808 | tf_op jit(solution)/shard_map/ppermute | solution.py:455
  7.6 5.2 %collective-permute-start.2 = (bf16[128,1792]{1,0:T(8,128)(2,1)S(1)}, bf16[128,1792]{1,0:T(8,128)(2,1)S(1)}, u32[]{:S(2)}, u32[]{:S(2)}) collective-permute-start(bf16[128,1792]{1,0:T(8,128)(2,1)S(1)} %get-tuple-element.32), channel_id=1, source_target_pairs={{0,16},{16,0},{32,48},{48,32},{64,80},{80,64},{96,112},{112,96},{1... | collective-permute-start | bytes 1376264 | tf_op jit(solution)/shard_map/ppermute | solution.py:319
  11.4 5.1 %collective-permute-start.6 = (bf16[128,1792]{1,0:T(8,128)(2,1)S(1)}, bf16[128,1792]{1,0:T(8,128)(2,1)S(1)}, u32[]{:S(2)}, u32[]{:S(2)}) collective-permute-start(bf16[128,1792]{1,0:T(8,128)(2,1)S(1)} %get-tuple-element.30), channel_id=1, source_target_pairs={{0,16},{16,0},{32,48},{48,32},{64,80},{80,64},{96,112},{112,96},{1... | collective-permute-start | bytes 1376264 | tf_op jit(solution)/shard_map/ppermute | solution.py:319
  13.6 19.4 %collective-permute-start.9 = (s16[3600,128]{1,0:T(8,128)(2,1)S(1)}, s16[3600,128]{1,0:T(8,128)(2,1)}, u32[]{:S(2)}, u32[]{:S(2)}) collective-permute-start(s16[3600,128]{1,0:T(8,128)(2,1)S(1)} %hop1.1.after.refs_0_), channel_id=1, source_target_pairs={{0,32},{16,240},{32,64},{48,16},{64,96},{80,48},{96,128},{112,80},... | collective-permute-start | bytes 2764808 | tf_op jit(solution)/shard_map/ppermute | solution.py:455
  15.4 14.7 %collective-permute-start.8 = (bf16[128,3584]{1,0:T(8,128)(2,1)}, bf16[128,3584]{1,0:T(8,128)(2,1)}, u32[]{:S(2)}, u32[]{:S(2)}) collective-permute-start(bf16[128,3584]{1,0:T(8,128)(2,1)} %get-tuple-element.21), channel_id=1, source_target_pairs={{0,16},{16,0},{32,48},{48,32},{64,80},{80,64},{96,112},{112,96},{1... | collective-permute-start | bytes 2752520 | tf_op jit(solution)/shard_map/ppermute | solution.py:319
  23.9 19.0 %collective-permute-start.14 = (s16[3600,128]{1,0:T(8,128)(2,1)S(1)}, s16[3600,128]{1,0:T(8,128)(2,1)}, u32[]{:S(2)}, u32[]{:S(2)}) collective-permute-start(s16[3600,128]{1,0:T(8,128)(2,1)S(1)} %hop2.1.refs_0_.after), channel_id=1, source_target_pairs={{0,32},{16,240},{32,64},{48,16},{64,96},{80,48},{96,128},{112,80},... | collective-permute-start | bytes 2764808 | tf_op jit(solution)/shard_map/ppermute | solution.py:455
  26.2 28.0 %collective-permute-start.13 = (bf16[128,5376]{1,0:T(8,128)(2,1)}, bf16[128,5376]{1,0:T(8,128)(2,1)}, u32[]{:S(2)}, u32[]{:S(2)}) collective-permute-start(bf16[128,5376]{1,0:T(8,128)(2,1)} %get-tuple-element.23), channel_id=1, source_target_pairs={{0,16},{16,0},{32,48},{48,32},{64,80},{80,64},{96,112},{112,96},{1... | collective-permute-start | bytes 4128776 | tf_op jit(solution)/shard_map/ppermute | solution.py:319
  36.5 17.7 %collective-permute-start.15 = (s16[3600,128]{1,0:T(8,128)(2,1)S(1)}, s16[3600,128]{1,0:T(8,128)(2,1)S(1)}, u32[]{:S(2)}, u32[]{:S(2)}) collective-permute-start(s16[3600,128]{1,0:T(8,128)(2,1)S(1)} %hop3.1.after.refs_0_), channel_id=1, source_target_pairs={{0,32},{16,240},{32,64},{48,16},{64,96},{80,48},{96,128},{112,80},... | collective-permute-start | bytes 2764808 | tf_op jit(solution)/shard_map/ppermute | solution.py:455
  45.0 17.5 %collective-permute-start.17 = (s16[3600,128]{1,0:T(8,128)(2,1)S(1)}, s16[3600,128]{1,0:T(8,128)(2,1)S(1)}, u32[]{:S(2)}, u32[]{:S(2)}) collective-permute-start(s16[3600,128]{1,0:T(8,128)(2,1)S(1)} %hop4.1.refs_0_), channel_id=1, source_target_pairs={{0,32},{16,240},{32,64},{48,16},{64,96},{80,48},{96,128},{112,80},... | collective-permute-start | bytes 2764808 | tf_op jit(solution)/shard_map/ppermute | solution.py:455
  45.1 5.0 %collective-permute-start.3 = (f32[28,128]{1,0:T(8,128)S(1)}, f32[28,128]{1,0:T(8,128)S(1)}, u32[]{:S(2)}, u32[]{:S(2)}) collective-permute-start(f32[28,128]{1,0:T(8,128)S(1)} %get-tuple-element.18.k0), channel_id=1, source_target_pairs={{0,1},{1,2},{2,3},{3,0},{4,5},{5,6},{6,7},{7,4},{8,9},{9,10},{10,1... | collective-permute-start | bytes 43016 | tf_op jit(solution)/shard_map/ppermute | solution.py:396
  46.7 5.3 %collective-permute-start.4 = (f32[28,128]{1,0:T(8,128)S(1)}, f32[28,128]{1,0:T(8,128)S(1)}, u32[]{:S(2)}, u32[]{:S(2)}) collective-permute-start(f32[28,128]{1,0:T(8,128)S(1)} %get-tuple-element.18.k0), channel_id=1, source_target_pairs={{0,2},{1,3},{2,0},{3,1},{4,6},{5,7},{6,4},{7,5},{8,10},{9,11},{10,... | collective-permute-start | bytes 43016 | tf_op jit(solution)/shard_map/ppermute | solution.py:396
  50.1 3.9 %collective-permute-start.5 = (f32[28,128]{1,0:T(8,128)S(1)}, f32[28,128]{1,0:T(8,128)S(1)}, u32[]{:S(2)}, u32[]{:S(2)}) collective-permute-start(f32[28,128]{1,0:T(8,128)S(1)} %get-tuple-element.18.k0), channel_id=1, source_target_pairs={{0,3},{1,0},{2,1},{3,2},{4,7},{5,4},{6,5},{7,6},{8,11},{9,8},{10,9... | collective-permute-start | bytes 43016 | tf_op jit(solution)/shard_map/ppermute | solution.py:396
  56.1 17.1 %collective-permute-start.16 = (s16[3600,128]{1,0:T(8,128)(2,1)S(1)}, s16[3600,128]{1,0:T(8,128)(2,1)S(1)}, u32[]{:S(2)}, u32[]{:S(2)}) collective-permute-start(s16[3600,128]{1,0:T(8,128)(2,1)S(1)} %hop5.1.refs_0_), channel_id=1, source_target_pairs={{0,48},{16,224},{32,80},{48,0},{64,112},{80,32},{96,144},{112,64},... | collective-permute-start | bytes 2764808 | tf_op jit(solution)/shard_map/ppermute | solution.py:455
  64.4 17.9 %collective-permute-start.18 = (s16[3600,128]{1,0:T(8,128)(2,1)S(1)}, s16[3600,128]{1,0:T(8,128)(2,1)S(1)}, u32[]{:S(2)}, u32[]{:S(2)}) collective-permute-start(s16[3600,128]{1,0:T(8,128)(2,1)S(1)} %hop6.1), channel_id=1, source_target_pairs={{0,32},{16,240},{32,64},{48,16},{64,96},{80,48},{96,128},{112,80},... | collective-permute-start | bytes 2764808 | tf_op jit(solution)/shard_map/ppermute | solution.py:455
  64.5 4.3 %collective-permute-start.10 = (f32[4,28,128]{2,1,0:T(8,128)S(1)}, f32[4,28,128]{2,1,0:T(8,128)S(1)}, u32[]{:S(2)}, u32[]{:S(2)}) collective-permute-start(f32[4,28,128]{2,1,0:T(8,128)S(1)} %places.1.refs_1_.n0), channel_id=1, source_target_pairs={{0,4},{1,5},{2,6},{3,7},{4,8},{5,9},{6,10},{7,11},{8,12},{9,13},{1... | collective-permute-start | bytes 172040 | tf_op jit(solution)/shard_map/ppermute | solution.py:399
  64.8 5.9 %collective-permute-start.11 = (f32[4,28,128]{2,1,0:T(8,128)S(1)}, f32[4,28,128]{2,1,0:T(8,128)S(1)}, u32[]{:S(2)}, u32[]{:S(2)}) collective-permute-start(f32[4,28,128]{2,1,0:T(8,128)S(1)} %places.1.refs_1_.n0), channel_id=1, source_target_pairs={{0,8},{1,9},{2,10},{3,11},{4,12},{5,13},{6,14},{7,15},{8,0},{9,1},... | collective-permute-start | bytes 172040 | tf_op jit(solution)/shard_map/ppermute | solution.py:399
  67.3 5.9 %collective-permute-start.12 = (f32[4,28,128]{2,1,0:T(8,128)S(1)}, f32[4,28,128]{2,1,0:T(8,128)S(1)}, u32[]{:S(2)}, u32[]{:S(2)}) collective-permute-start(f32[4,28,128]{2,1,0:T(8,128)S(1)} %places.1.refs_1_.n0), channel_id=1, source_target_pairs={{0,12},{1,13},{2,14},{3,15},{4,0},{5,1},{6,2},{7,3},{8,4},{9,5},{1... | collective-permute-start | bytes 172040 | tf_op jit(solution)/shard_map/ppermute | solution.py:399
  83.4 8.8 %collective-permute-start.19 = (f32[28,128]{1,0:T(8,128)S(1)}, f32[28,128]{1,0:T(8,128)S(1)}, u32[]{:S(2)}, u32[]{:S(2)}) collective-permute-start(f32[28,128]{1,0:T(8,128)S(1)} %get-tuple-element.27.kept.k0), channel_id=1, source_target_pairs={{0,1},{1,2},{2,3},{3,0},{4,5},{5,6},{6,7},{7,4},{8,9},{9,10},{10,1... | collective-permute-start | bytes 43016 | tf_op jit(solution)/shard_map/ppermute | solution.py:396
  85.0 7.3 %collective-permute-start.20 = (f32[28,128]{1,0:T(8,128)S(1)}, f32[28,128]{1,0:T(8,128)S(1)}, u32[]{:S(2)}, u32[]{:S(2)}) collective-permute-start(f32[28,128]{1,0:T(8,128)S(1)} %get-tuple-element.27.kept.k0), channel_id=1, source_target_pairs={{0,2},{1,3},{2,0},{3,1},{4,6},{5,7},{6,4},{7,5},{8,10},{9,11},{10,... | collective-permute-start | bytes 43016 | tf_op jit(solution)/shard_map/ppermute | solution.py:396
  87.7 4.5 %collective-permute-start.21 = (f32[28,128]{1,0:T(8,128)S(1)}, f32[28,128]{1,0:T(8,128)S(1)}, u32[]{:S(2)}, u32[]{:S(2)}) collective-permute-start(f32[28,128]{1,0:T(8,128)S(1)} %get-tuple-element.27.kept.k0), channel_id=1, source_target_pairs={{0,3},{1,0},{2,1},{3,2},{4,7},{5,4},{6,5},{7,6},{8,11},{9,8},{10,9... | collective-permute-start | bytes 43016 | tf_op jit(solution)/shard_map/ppermute | solution.py:396
  92.4 4.3 %collective-permute-start.22 = (f32[4,28,128]{2,1,0:T(8,128)S(1)}, f32[4,28,128]{2,1,0:T(8,128)S(1)}, u32[]{:S(2)}, u32[]{:S(2)}) collective-permute-start(f32[4,28,128]{2,1,0:T(8,128)S(1)} %arrange.1.k0), channel_id=1, source_target_pairs={{0,4},{1,5},{2,6},{3,7},{4,8},{5,9},{6,10},{7,11},{8,12},{9,13},{1... | collective-permute-start | bytes 172040 | tf_op jit(solution)/shard_map/ppermute | solution.py:399
  92.7 5.8 %collective-permute-start.23 = (f32[4,28,128]{2,1,0:T(8,128)S(1)}, f32[4,28,128]{2,1,0:T(8,128)S(1)}, u32[]{:S(2)}, u32[]{:S(2)}) collective-permute-start(f32[4,28,128]{2,1,0:T(8,128)S(1)} %arrange.1.k0), channel_id=1, source_target_pairs={{0,8},{1,9},{2,10},{3,11},{4,12},{5,13},{6,14},{7,15},{8,0},{9,1},... | collective-permute-start | bytes 172040 | tf_op jit(solution)/shard_map/ppermute | solution.py:399
  95.3 5.5 %collective-permute-start.24 = (f32[4,28,128]{2,1,0:T(8,128)S(1)}, f32[4,28,128]{2,1,0:T(8,128)S(1)}, u32[]{:S(2)}, u32[]{:S(2)}) collective-permute-start(f32[4,28,128]{2,1,0:T(8,128)S(1)} %arrange.1.k0), channel_id=1, source_target_pairs={{0,12},{1,13},{2,14},{3,15},{4,0},{5,1},{6,2},{7,3},{8,4},{9,5},{1... | collective-permute-start | bytes 172040 | tf_op jit(solution)/shard_map/ppermute | solution.py:399
  (11 other events, 65.6 us)
